TPU v7x, 256 devices: a whole 4x4x8 slice. The times are simulated.
256 devices in a mesh: rep: 8 (over x, core), row: 8 (over z), col: 4 (over y).
Axes of the slice: x: 4, y: 4, z: 8, core: 2. Of those that a mesh axis runs over, the one named last changes fastest.
Arguments:
- grad_parts: bfloat16 [8, 2, 8, 512, 14336], P('rep', None, None, 'row', 'col'), may hold values from -100 to 100, as said below
- weights: float32 [2, 4096, 14336], P(None, ('rep', 'row'), 'col'), may hold values from -1.5 to 1.5
Outputs:
- updated: float32 [2, 4096, 14336], P(None, ('rep', 'row'), 'col')
- direction: float32 [2, 4096, 14336], P(None, ('rep', 'row'), 'col')
Inputs may be any that keep to these rules, and one draw needn't show every extreme that they name: `grad_parts`: finite partial gradients.
All inputs are finite; a program needn't handle non-finite values.
Results may differ from a plain program's by a relative error of at most 0.0003.
Values sent between devices are 32-bit elements; how exact they have to be, the bound alone decides.
No kernel may reach another device: no remote copies, remote signals or barrier semaphores. Data moves between devices by JAX's collectives and lax.ppermute only.
A program may use at most 128 MiB of HBM per device.

v0:
```python
import jax
import jax.numpy as jnp
from jax import lax
from jax.sharding import PartitionSpec as P

DW = 4096
FW = 14336
ITERS = 5


EPSILON = 1e-06
LEARNING_RATE = 0.02
DECAY_RATE = 0.1


def normalize(values):
    for sweep in range(ITERS):
        row_part = jnp.sum(values * values, axis=2)
        row_total = lax.psum(row_part, "col")
        values = values * lax.rsqrt(row_total / FW + EPSILON)[:, :, None]
        column_part = jnp.sum(values * values, axis=1)
        column_total = lax.psum(column_part, ("rep", "row"))
        factor = lax.rsqrt(column_total / DW + EPSILON)
        values = values * factor[:, None, :]
    return values


def per_device(grad_parts, weights):
    pieces = []
    for matrix in range(2):
        summed = lax.psum_scatter(
            grad_parts[0, matrix].astype(jnp.float32), "rep", scatter_dimension=0, tiled=True
        )
        pieces.append(normalize(summed))
    direction = jnp.concatenate(pieces, axis=0)
    updated = weights * (1.0 - LEARNING_RATE * DECAY_RATE) - LEARNING_RATE * direction
    return (updated, direction)


def solution(mesh):
    in_specs = (P("rep", None, None, "row", "col"), P(None, ("rep", "row"), "col"))
    out_specs = (P(None, ("rep", "row"), "col"), P(None, ("rep", "row"), "col"))
    return jax.shard_map(
        per_device, mesh=mesh, in_specs=in_specs, out_specs=out_specs, check_vma=False
    )
```

profile of v0, /device:TPU:1, one launch (start us, length us, event | category | flops | bytes accessed | tf_op | source)
XLA Modules:
  0.0 1411.3 jit_solution(8219511427940111641)
XLA Ops:
  7.2 10.4 bitcast_convert_fusion.1
  17.7 0.7 reduce-scatter.3.cloned.1.call-update
  18.4 52.6 %reduce-scatter.5.cloned.1.call-done = f32[1,64,3584]{2,1,0:T(8,128)} async-done(((f32[8,64,3584]{2,1,0:T(8,128)}), f32[1,64,3584]{2,1,0:T(8,128)}) %reduce-scatter.5.cloned.1.call-update) | async-done | bytes 917520 | tf_op jit(solution)/shard_map/reduce_scatter | solution.py:31
  71.0 1.4 multiply_reduce_fusion.9
  72.4 50.8 %reduce-scatter.3.cloned.1.call-done = f32[1,64,3584]{2,1,0:T(8,128)} async-done(((f32[8,64,3584]{2,1,0:T(8,128)}), f32[1,64,3584]{2,1,0:T(8,128)}) %reduce-scatter.3.cloned.1.call-update) | async-done | bytes 917520 | tf_op jit(solution)/shard_map/reduce_scatter | solution.py:31
  123.2 1.4 multiply_reduce_fusion.19
  124.7 8.5 all-reduce.9
  133.6 242.1 %all-reduce.4 = (f32[1,3584]{1,0:T(1,128)S(1)}, f32[1,3584]{1,0:T(1,128)S(1)}) all-reduce(f32[1,3584]{1,0:T(1,128)S(1)} %reduce_sum.243, f32[1,3584]{1,0:T(1,128)S(1)} %reduce_sum.223), channel_id=1, replica_groups=mesh['rep'=8,'row'=8,'col'=4] {'rep','row'}, use_global_device_ids=true, to_apply=%region_25.0 | all-reduce | flops 7168 | bytes 57344 | tf_op jit(solution)/shard_map/psum | solution.py:22
  375.7 0.3 multiply_reduce_fusion.7
  376.0 0.3 multiply_reduce_fusion.17
  376.3 6.0 all-reduce.8
  382.3 0.2 multiply_reduce_fusion.16
  382.9 248.0 %all-reduce.3 = (f32[1,3584]{1,0:T(1,128)S(1)}, f32[1,3584]{1,0:T(1,128)S(1)}) all-reduce(f32[1,3584]{1,0:T(1,128)S(1)} %reduce_sum.247, f32[1,3584]{1,0:T(1,128)S(1)} %reduce_sum.227), channel_id=1, replica_groups=mesh['rep'=8,'row'=8,'col'=4] {'rep','row'}, use_global_device_ids=true, to_apply=%region_29.0 | all-reduce | flops 7168 | bytes 57344 | tf_op jit(solution)/shard_map/psum | solution.py:22
  631.0 0.4 multiply_reduce_fusion.5
  631.4 0.4 multiply_reduce_fusion.15
  631.7 7.8 all-reduce.7
  640.0 248.1 %all-reduce.2 = (f32[1,3584]{1,0:T(1,128)S(1)}, f32[1,3584]{1,0:T(1,128)S(1)}) all-reduce(f32[1,3584]{1,0:T(1,128)S(1)} %reduce_sum.251, f32[1,3584]{1,0:T(1,128)S(1)} %reduce_sum.231), channel_id=1, replica_groups=mesh['rep'=8,'row'=8,'col'=4] {'rep','row'}, use_global_device_ids=true, to_apply=%region_33.0 | all-reduce | flops 7168 | bytes 57344 | tf_op jit(solution)/shard_map/psum | solution.py:22
  888.1 0.3 multiply_reduce_fusion.3
  888.4 0.3 multiply_reduce_fusion.13
  888.7 6.0 all-reduce.6
  894.8 0.2 multiply_reduce_fusion.12
  895.3 248.1 %all-reduce.1 = (f32[1,3584]{1,0:T(1,128)S(1)}, f32[1,3584]{1,0:T(1,128)S(1)}) all-reduce(f32[1,3584]{1,0:T(1,128)S(1)} %reduce_sum.255, f32[1,3584]{1,0:T(1,128)S(1)} %reduce_sum.235), channel_id=1, replica_groups=mesh['rep'=8,'row'=8,'col'=4] {'rep','row'}, use_global_device_ids=true, to_apply=%region_37.0 | all-reduce | flops 7168 | bytes 57344 | tf_op jit(solution)/shard_map/psum | solution.py:22
  1143.4 0.4 multiply_reduce_fusion.1
  1143.8 0.4 multiply_reduce_fusion.11
  1144.2 7.8 all-reduce.5
  1152.0 0.3 multiply_reduce_fusion.10
  1152.3 0.3 multiply_reduce_fusion
  1152.6 248.0 %all-reduce = (f32[1,3584]{1,0:T(1,128)S(1)}, f32[1,3584]{1,0:T(1,128)S(1)}) all-reduce(f32[1,3584]{1,0:T(1,128)S(1)} %reduce_sum.259, f32[1,3584]{1,0:T(1,128)S(1)} %reduce_sum.239), channel_id=1, replica_groups=mesh['rep'=8,'row'=8,'col'=4] {'rep','row'}, use_global_device_ids=true, to_apply=%region_41.0 | all-reduce | flops 7168 | bytes 57344 | tf_op jit(solution)/shard_map/psum | solution.py:22
  1400.7 0.3 multiply_multiply_fusion
  1401.0 0.3 multiply_multiply_fusion.5
  1401.3 0.9 copy-done.2
  1402.2 2.2 multiply_subtract_fusion
  (43 shorter events, 2.0 us)
Async XLA Ops:
  7.2 63.9 %reduce-scatter.5.cloned.1.call-start = ((), (), s32[]{:S(2)}) async-start(), calls=%async_computation.3 | async-start | bytes 8257536 | tf_op jit(solution)/shard_map/reduce_scatter | solution.py:31
  17.6 105.6 %reduce-scatter.3.cloned.1.call-start = ((), (), s32[]{:S(2)}) async-start(), calls=%async_computation.2 | async-start | bytes 8257536 | tf_op jit(solution)/shard_map/reduce_scatter | solution.py:31
  71.0 62.1 %copy-start = (f32[1,64,3584]{2,1,0:T(8,128)S(1)}, f32[1,64,3584]{2,1,0:T(8,128)}, u32[]{:S(2)}) copy-start(f32[1,64,3584]{2,1,0:T(8,128)} %reduce-scatter.5.cloned.1.call-done) | copy-start | bytes 2752516
  123.2 10.1 copy-start.1
  1400.7 1.5 copy-start.2
Sparse Core Ops, SparseCore 0:
  17.8 53.2 reduce-scatter.4
  73.6 49.6 reduce-scatter.2
where the time goes:
time: 1420 us; the launch traced here: 1410 us
  blocking collectives  1270 us (89%)
  waiting for transfers between devices  104 us (7%)
  other arithmetic  21.4 us (2%)
  between operations  14.3 us (1%)
    psum x5, blocking collectives, normalize(): column_total = lax.psum(column_part, ('rep', 'row'))  1230 us
    reduce_scatter x2, waiting for transfers between devices, per_device(): lax.psum_scatter(grad_parts[0, matrix].astype(jnp.float32), 'rep', scatte...  103 us
    psum x5, blocking collectives, normalize(): row_total = lax.psum(row_part, 'col')  36.1 us
  transfers between devices with their start and end apart: 2, of which 2 were waited for; matrix products, arithmetic and copies ran while one was open for 0% of the time, Pallas kernels for 0%

commit v1 on v0

v1 whole, which is shorter than its diff:
```python
import jax
import jax.numpy as jnp
from jax import lax
from jax.experimental import pallas as pl
from jax.experimental.pallas import tpu as pltpu
from jax.sharding import Mesh
from jax.sharding import PartitionSpec as P

DW = 4096
FW = 14336
ITERS = 5


EPSILON = 1e-06
LEARNING_RATE = 0.02
DECAY_RATE = 0.1


def widen_kernel(place, grads, first, second):
    first[0] = grads[0, 0, 0].astype(jnp.float32)
    second[0] = grads[1, 0, 0].astype(jnp.float32)


def widen_add_kernel(place, grads, other_first, other_second, first, second):
    first[0] = grads[0, 0, 0].astype(jnp.float32) + other_first[0]
    second[0] = grads[1, 0, 0].astype(jnp.float32) + other_second[0]


def widen(grads, place, others=()):
    _, groups, _, rows, columns = grads.shape
    width = columns // groups
    flat = pl.BlockSpec((1, rows, width), lambda j, place: (j, 0, 0))
    return pl.pallas_call(
        widen_add_kernel if others else widen_kernel,
        grid_spec=pltpu.PrefetchScalarGridSpec(
            num_scalar_prefetch=1,
            grid=(groups,),
            in_specs=[
                pl.BlockSpec(
                    (2, 1, 1, rows, width), lambda j, place: (0, j, place[0], 0, place[1])
                )
            ]
            + [flat] * len(others),
            out_specs=[flat, flat],
        ),
        out_shape=[jax.ShapeDtypeStruct((groups, rows, width), jnp.float32)] * 2,
    )(place, grads, *others)


def reduce_scatter(grads, size):
    x = lax.axis_index("x")
    core = lax.axis_index("core")

    def place(which, step):
        return jnp.stack([which, lax.rem(x + step, size)]).astype(jnp.int32)

    def move(values, step):
        return lax.ppermute(values, "x", [(i, (i + step) % size) for i in range(size)])

    total = {}
    for step in (2, 1, 3, 0):
        sent = widen(grads, place(1 - core, step))
        other = [lax.ppermute(s, "core", [(0, 1), (1, 0)]) for s in sent]
        total[step] = widen(grads, place(core, step), other)
    right = move(total[2][0], 1)
    left = move(total[2][1], -1)
    right_plain = move(total[1][1], 1)
    left_plain = move(total[3][0], -1)
    right_summed = move(total[1][0] + right, 1)
    left_summed = move(total[3][1] + left, -1)
    return (
        total[0][0] + left_plain + right_summed,
        total[0][1] + right_plain + left_summed,
    )


def group_sum(parts, axes, size):
    flat = jnp.concatenate(parts)[None, :]
    spread = jnp.broadcast_to(flat[None], (size,) + flat.shape)
    total = jnp.sum(lax.all_to_all(spread, axes, 0, 0, tiled=True), axis=(0, 1))
    return jnp.split(total, 2)


def per_device(sizes, grad_parts, weights):
    size_x, size_core, size_row, size_col = sizes
    _, _, blocks, rows, columns = grad_parts.shape
    grads = grad_parts.reshape(2, size_x, size_core, rows, columns)
    summed = reduce_scatter(grads, size_x)
    width = columns // size_x
    values = [s.reshape(size_x * rows, width) for s in summed]
    for sweep in range(ITERS):
        totals = group_sum(
            [jnp.sum(v * v, axis=1) for v in values], ("x", "col"), size_x * size_col
        )
        values = [v * lax.rsqrt(t / FW + EPSILON)[:, None] for v, t in zip(values, totals)]
        totals = group_sum(
            [jnp.sum(v * v, axis=0) for v in values], ("core", "row"), size_core * size_row
        )
        values = [v * lax.rsqrt(t / DW + EPSILON)[None, :] for v, t in zip(values, totals)]
    direction = jnp.stack([v.reshape(size_x, rows, width) for v in values], axis=1)
    direction = lax.all_to_all(direction, "x", 0, 0, tiled=True)
    direction = direction.transpose(1, 2, 0, 3).reshape(2, rows, columns)
    updated = weights * (1.0 - LEARNING_RATE * DECAY_RATE) - LEARNING_RATE * direction
    return (updated, direction)


def solution(mesh):
    size_core = 2
    size_x = mesh.shape["rep"] // size_core
    sizes = (size_x, size_core, mesh.shape["row"], mesh.shape["col"])
    split = Mesh(mesh.devices.reshape(sizes), ("x", "core", "row", "col"))
    rep = ("x", "core")
    in_specs = (P(rep, None, None, "row", "col"), P(None, rep + ("row",), "col"))
    out_specs = (P(None, rep + ("row",), "col"), P(None, rep + ("row",), "col"))

    def run(grad_parts, weights):
        return per_device(sizes, grad_parts, weights)

    return jax.shard_map(
        run, mesh=split, in_specs=in_specs, out_specs=out_specs, check_vma=False
    )
```

time: 1420 us -> 252 us (0.18)
  blocking collectives: 1270 us -> 140 us
  waiting for transfers between devices: 104 us -> 34.1 us
  Pallas kernels: 0 us -> 35 us
    psum x10 -> x0, blocking collectives: 1270 us -> none  [the longest x5 1230 us: normalize(): column_total = lax.psum(column_part, ('rep', 'row'))]
    all_to_all x0 -> x11, blocking collectives: none -> 140 us  [the longest x10 115 us: group_sum(): total = jnp.sum(lax.all_to_all(spread, axes, 0, 0, tiled=True), axis=(0, 1))]
    reduce_scatter x2 -> x0, waiting for transfers between devices: 103 us -> none  [per_device(): lax.psum_scatter(grad_parts[0, matrix].astype(jnp.float32), 'rep', scatte...]
    pallas_call x0 -> x8, Pallas kernels: none -> 35 us  [widen(): pl.pallas_call(widen_add_kernel if others else widen_kernel, grid_spec=pl...]
    ppermute x0 -> x14, waiting for transfers between devices: none -> 34.1 us  [the longest x6 34.1 us: move(): lax.ppermute(values, 'x', [(i, (i + step) % size) for i in range(size)])]
  transfers between devices with their start and end apart: 2 -> 14, of which waited for: 2 -> 4; matrix products, arithmetic and copies ran while one was open for 0% -> 4% of each run, Pallas kernels for 0% -> 12%
where the time goes in v1:
time: 252 us; the launch traced here: 250 us
  blocking collectives  140 us (56%)
  Pallas kernels  35 us (14%)
  waiting for transfers between devices  34.1 us (14%)
  other arithmetic  21.4 us (8%)
  starting transfers between devices  10.4 us (4%)
  local copies, waits for them, and re-layouts  7.92 us (3%)
    all_to_all x10, blocking collectives, group_sum(): total = jnp.sum(lax.all_to_all(spread, axes, 0, 0, tiled=True), axis=(0, 1))  115 us
    pallas_call x8, Pallas kernels, widen(): pl.pallas_call(widen_add_kernel if others else widen_kernel, grid_spec=pl...  35 us
    ppermute x6, waiting for transfers between devices, move(): lax.ppermute(values, 'x', [(i, (i + step) % size) for i in range(size)])  34.1 us
    all_to_all x1, blocking collectives, per_device(): direction = lax.all_to_all(direction, 'x', 0, 0, tiled=True)  24.9 us
    reduce_sum x10, other arithmetic, per_device(): jnp.sum(v * v, axis=1)  6.69 us
    unnamed x16, local copies, waits for them, and re-layouts  5.51 us
    ppermute x6, starting transfers between devices, move(): lax.ppermute(values, 'x', [(i, (i + step) % size) for i in range(size)])  5.45 us
  transfers between devices with their start and end apart: 14, of which 4 were waited for; matrix products, arithmetic and copies ran while one was open for 4% of the time, Pallas kernels for 12%

profile of v1, /device:TPU:1, one launch (start us, length us, event | category | flops | bytes accessed | tf_op | source)
XLA Modules:
  0.0 250.1 jit_solution(2017365710494080855)
XLA Ops:
  1.3 4.2 %shard_map.47 = (f32[4,64,896]{2,1,0:T(8,128)}, f32[4,64,896]{2,1,0:T(8,128)}) custom-call(s32[2]{0:T(128)} %get-tuple-element.61.place, bf16[2,4,2,64,3584]{4,3,2,1,0:T(8,128)(2,1)} %bitcast.14), custom_call_target="tpu_custom_call" | custom-call | tf_op jit(solution)/shard_map/pallas_call | solution.py:33
  5.5 3.2 %collective-permute-start.7 = (f32[4,64,896]{2,1,0:T(8,128)}, f32[4,64,896]{2,1,0:T(8,128)S(1)}, u32[]{:S(2)}, u32[]{:S(2)}) collective-permute-start(f32[4,64,896]{2,1,0:T(8,128)} %get-tuple-element.27), channel_id=1, source_target_pairs={{0,32},{32,0},{1,33},{33,1},{2,34},{34,2},{3,35},{35,3},{4,36},{36... | collective-permute-start | bytes 2752520 | tf_op jit(solution)/shard_map/ppermute | solution.py:63
  9.3 4.2 %shard_map.43 = (f32[4,64,896]{2,1,0:T(8,128)}, f32[4,64,896]{2,1,0:T(8,128)}) custom-call(s32[2]{0:T(128)} %get-tuple-element.59.place, bf16[2,4,2,64,3584]{4,3,2,1,0:T(8,128)(2,1)} %bitcast.15), custom_call_target="tpu_custom_call" | custom-call | tf_op jit(solution)/shard_map/pallas_call | solution.py:33
  14.0 4.2 %shard_map.45 = (f32[4,64,896]{2,1,0:T(8,128)}, f32[4,64,896]{2,1,0:T(8,128)}) custom-call(s32[2]{0:T(128)} %get-tuple-element.60.place, bf16[2,4,2,64,3584]{4,3,2,1,0:T(8,128)(2,1)} %bitcast.16), custom_call_target="tpu_custom_call" | custom-call | tf_op jit(solution)/shard_map/pallas_call | solution.py:33
  21.2 4.6 %shard_map.48 = (f32[4,64,896]{2,1,0:T(8,128)}, f32[4,64,896]{2,1,0:T(8,128)}) custom-call(s32[2]{0:T(128)} %pad_add_fusion.7.place, bf16[2,4,2,64,3584]{4,3,2,1,0:T(8,128)(2,1)} %bitcast.17, f32[4,64,896]{2,1,0:T(8,128)} %copy-done.3, f32[4,64,896]{2,1,0:T(8,128)} %copy-done.5), custom_call_target="tpu_custom_call" | custom-call | tf_op jit(solution)/shard_map/pallas_call | solution.py:33
  25.8 2.7 %collective-permute-start.12 = (f32[4,64,896]{2,1,0:T(8,128)}, f32[4,64,896]{2,1,0:T(8,128)}, u32[]{:S(2)}, u32[]{:S(2)}) collective-permute-start(f32[4,64,896]{2,1,0:T(8,128)} %get-tuple-element.33), channel_id=1, source_target_pairs={{0,192},{64,0},{128,64},{192,128},{1,193},{65,1},{129,65},{193,129... | collective-permute-start | bytes 2752520 | tf_op jit(solution)/shard_map/ppermute | solution.py:58
  28.5 4.2 %shard_map.41 = (f32[4,64,896]{2,1,0:T(8,128)}, f32[4,64,896]{2,1,0:T(8,128)}) custom-call(s32[2]{0:T(128)} %get-tuple-element.58.place, bf16[2,4,2,64,3584]{4,3,2,1,0:T(8,128)(2,1)} %bitcast.18), custom_call_target="tpu_custom_call" | custom-call | tf_op jit(solution)/shard_map/pallas_call | solution.py:33
  34.5 4.6 %shard_map.44 = (f32[4,64,896]{2,1,0:T(8,128)}, f32[4,64,896]{2,1,0:T(8,128)}) custom-call(s32[2]{0:T(128)} %pad_add_fusion.3.place, bf16[2,4,2,64,3584]{4,3,2,1,0:T(8,128)(2,1)} %bitcast.19, f32[4,64,896]{2,1,0:T(8,128)} %collective-permute-done.2.other_first, f32[4,64,896]{2,1,0:T(8,128)} %collective-permute-done.3.other_second), custom_call_target="tpu_custom_call" | custom-call | tf_op jit(solution)/shard_map/pallas_call | solution.py:33
  40.0 4.6 %shard_map.46 = (f32[4,64,896]{2,1,0:T(8,128)}, f32[4,64,896]{2,1,0:T(8,128)}) custom-call(s32[2]{0:T(128)} %pad_add_fusion.5.place, bf16[2,4,2,64,3584]{4,3,2,1,0:T(8,128)(2,1)} %bitcast.20, f32[4,64,896]{2,1,0:T(8,128)} %copy-done.2, f32[4,64,896]{2,1,0:T(8,128)} %collective-permute-done.6.other_second), custom_call_target="tpu_custom_call" | custom-call | tf_op jit(solution)/shard_map/pallas_call | solution.py:33
  44.6 4.7 %collective-permute-done.9 = f32[4,64,896]{2,1,0:T(8,128)} collective-permute-done((f32[4,64,896]{2,1,0:T(8,128)}, f32[4,64,896]{2,1,0:T(8,128)}, u32[]{:S(2)}, u32[]{:S(2)}) %collective-permute-start.9) | collective-permute-done | bytes 917536 | tf_op jit(solution)/shard_map/ppermute | solution.py:58
  49.3 2.5 %add.114 = f32[4,64,896]{2,1,0:T(8,128)} add(f32[4,64,896]{2,1,0:T(8,128)} %get-tuple-element.26, f32[4,64,896]{2,1,0:T(8,128)} %collective-permute-done.9) | non-fusion elementwise | flops 229376 | bytes 2752512 | tf_op jit(solution)/shard_map/add | solution.py:69
  51.9 2.2 add.117
  54.1 2.7 %collective-permute-start.13 = (f32[4,64,896]{2,1,0:T(8,128)}, f32[4,64,896]{2,1,0:T(8,128)}, u32[]{:S(2)}, u32[]{:S(2)}) collective-permute-start(f32[4,64,896]{2,1,0:T(8,128)} %add.117), channel_id=1, source_target_pairs={{0,192},{64,0},{128,64},{192,128},{1,193},{65,1},{129,65},{193,129... | collective-permute-start | bytes 2752520 | tf_op jit(solution)/shard_map/ppermute | solution.py:58
  58.4 4.6 %shard_map.42 = (f32[4,64,896]{2,1,0:T(8,128)}, f32[4,64,896]{2,1,0:T(8,128)}) custom-call(s32[2]{0:T(128)} %pad_add_fusion.1.place, bf16[2,4,2,64,3584]{4,3,2,1,0:T(8,128)(2,1)} %bitcast.21, f32[4,64,896]{2,1,0:T(8,128)} %copy-done.4, f32[4,64,896]{2,1,0:T(8,128)} %copy-done.6), custom_call_target="tpu_custom_call" | custom-call | tf_op jit(solution)/shard_map/pallas_call | solution.py:33
  63.0 4.9 %collective-permute-done.4 = f32[4,64,896]{2,1,0:T(8,128)} collective-permute-done((f32[4,64,896]{2,1,0:T(8,128)}, f32[4,64,896]{2,1,0:T(8,128)}, u32[]{:S(2)}, u32[]{:S(2)}) %collective-permute-start.4) | collective-permute-done | bytes 917536 | tf_op jit(solution)/shard_map/ppermute | solution.py:58
  67.9 6.4 %collective-permute-done.10 = f32[4,64,896]{2,1,0:T(8,128)S(1)} collective-permute-done((f32[4,64,896]{2,1,0:T(8,128)}, f32[4,64,896]{2,1,0:T(8,128)S(1)}, u32[]{:S(2)}, u32[]{:S(2)}) %collective-permute-start.10) | collective-permute-done | bytes 917536 | tf_op jit(solution)/shard_map/ppermute | solution.py:58
  74.4 1.7 multiply_reduce_fusion.19
  76.1 18.0 %collective-permute-done.11 = f32[4,64,896]{2,1,0:T(8,128)} collective-permute-done((f32[4,64,896]{2,1,0:T(8,128)}, f32[4,64,896]{2,1,0:T(8,128)}, u32[]{:S(2)}, u32[]{:S(2)}) %collective-permute-start.11) | collective-permute-done | bytes 917536 | tf_op jit(solution)/shard_map/ppermute | solution.py:58
  94.1 1.9 multiply_reduce_fusion.18
  96.2 9.0 %all_to_all.55 = f32[16,1,512]{2,1,0:T(1,128)S(1)} all-to-all(f32[16,1,512]{2,1,0:T(1,128)S(1)} %broadcast_in_dim.20), channel_id=1, replica_groups=mesh['x'=4,'core'=2,'row'=8,'col'=4] {'x','col'}, dimensions={0} | all-to-all | bytes 65536 | tf_op jit(solution)/shard_map/all_to_all | solution.py:80
  105.9 18.5 %all_to_all.56 = f32[16,1,1792]{2,1,0:T(1,128)S(1)} all-to-all(f32[16,1,1792]{2,1,0:T(1,128)S(1)} %broadcast_in_dim.21), channel_id=1, replica_groups=mesh['x'=4,'core'=2,'row'=8,'col'=4] {'core','row'}, dimensions={0} | all-to-all | bytes 229376 | tf_op jit(solution)/shard_map/all_to_all | solution.py:80
  125.3 9.3 %all_to_all.57 = f32[16,1,512]{2,1,0:T(1,128)S(1)} all-to-all(f32[16,1,512]{2,1,0:T(1,128)S(1)} %broadcast_in_dim.22), channel_id=1, replica_groups=mesh['x'=4,'core'=2,'row'=8,'col'=4] {'x','col'}, dimensions={0} | all-to-all | bytes 65536 | tf_op jit(solution)/shard_map/all_to_all | solution.py:80
  135.3 12.7 %all_to_all.58 = f32[16,1,1792]{2,1,0:T(1,128)S(1)} all-to-all(f32[16,1,1792]{2,1,0:T(1,128)S(1)} %broadcast_in_dim.23), channel_id=1, replica_groups=mesh['x'=4,'core'=2,'row'=8,'col'=4] {'core','row'}, dimensions={0} | all-to-all | bytes 229376 | tf_op jit(solution)/shard_map/all_to_all | solution.py:80
  149.0 9.3 %all_to_all.59 = f32[16,1,512]{2,1,0:T(1,128)S(1)} all-to-all(f32[16,1,512]{2,1,0:T(1,128)S(1)} %broadcast_in_dim.24), channel_id=1, replica_groups=mesh['x'=4,'core'=2,'row'=8,'col'=4] {'x','col'}, dimensions={0} | all-to-all | bytes 65536 | tf_op jit(solution)/shard_map/all_to_all | solution.py:80
  159.2 12.7 %all_to_all.60 = f32[16,1,1792]{2,1,0:T(1,128)S(1)} all-to-all(f32[16,1,1792]{2,1,0:T(1,128)S(1)} %broadcast_in_dim.25), channel_id=1, replica_groups=mesh['x'=4,'core'=2,'row'=8,'col'=4] {'core','row'}, dimensions={0} | all-to-all | bytes 229376 | tf_op jit(solution)/shard_map/all_to_all | solution.py:80
  173.0 9.3 %all_to_all.61 = f32[16,1,512]{2,1,0:T(1,128)S(1)} all-to-all(f32[16,1,512]{2,1,0:T(1,128)S(1)} %broadcast_in_dim.26), channel_id=1, replica_groups=mesh['x'=4,'core'=2,'row'=8,'col'=4] {'x','col'}, dimensions={0} | all-to-all | bytes 65536 | tf_op jit(solution)/shard_map/all_to_all | solution.py:80
  183.3 12.7 %all_to_all.62 = f32[16,1,1792]{2,1,0:T(1,128)S(1)} all-to-all(f32[16,1,1792]{2,1,0:T(1,128)S(1)} %broadcast_in_dim.27), channel_id=1, replica_groups=mesh['x'=4,'core'=2,'row'=8,'col'=4] {'core','row'}, dimensions={0} | all-to-all | bytes 229376 | tf_op jit(solution)/shard_map/all_to_all | solution.py:80
  197.3 9.3 %all_to_all.63 = f32[16,1,512]{2,1,0:T(1,128)S(1)} all-to-all(f32[16,1,512]{2,1,0:T(1,128)S(1)} %broadcast_in_dim.28), channel_id=1, replica_groups=mesh['x'=4,'core'=2,'row'=8,'col'=4] {'x','col'}, dimensions={0} | all-to-all | bytes 65536 | tf_op jit(solution)/shard_map/all_to_all | solution.py:80
  207.7 12.7 %all_to_all.64 = f32[16,1,1792]{2,1,0:T(1,128)S(1)} all-to-all(f32[16,1,1792]{2,1,0:T(1,128)S(1)} %broadcast_in_dim.29), channel_id=1, replica_groups=mesh['x'=4,'core'=2,'row'=8,'col'=4] {'core','row'}, dimensions={0} | all-to-all | bytes 229376 | tf_op jit(solution)/shard_map/all_to_all | solution.py:80
  221.6 24.9 %all_to_all.65 = f32[4,2,64,896]{3,2,1,0:T(8,128)S(1)} all-to-all(f32[4,2,64,896]{3,2,1,0:T(8,128)S(1)} %copy.19), channel_id=1, replica_groups=mesh['x'=4,'core'=2,'row'=8,'col'=4] {'x'}, dimensions={0} | all-to-all | bytes 3670016 | tf_op jit(solution)/shard_map/all_to_all | solution.py:101
  246.7 1.9 copy-done.1
  248.6 1.5 multiply_subtract_fusion
  (125 shorter events, 19.3 us)
Async XLA Ops:
  5.5 13.9 %collective-permute-start.7 = (f32[4,64,896]{2,1,0:T(8,128)}, f32[4,64,896]{2,1,0:T(8,128)S(1)}, u32[]{:S(2)}, u32[]{:S(2)}) collective-permute-start(f32[4,64,896]{2,1,0:T(8,128)} %get-tuple-element.27), channel_id=1, source_target_pairs={{0,32},{32,0},{1,33},{33,1},{2,34},{34,2},{3,35},{35,3},{4,36},{36... | collective-permute-start | bytes 2752520 | tf_op jit(solution)/shard_map/ppermute | solution.py:63
  8.7 10.6 %collective-permute-start.8 = (f32[4,64,896]{2,1,0:T(8,128)}, f32[4,64,896]{2,1,0:T(8,128)S(1)}, u32[]{:S(2)}, u32[]{:S(2)}) collective-permute-start(f32[4,64,896]{2,1,0:T(8,128)} %get-tuple-element.28), channel_id=1, source_target_pairs={{0,32},{32,0},{1,33},{33,1},{2,34},{34,2},{3,35},{35,3},{4,36},{36... | collective-permute-start | bytes 2752520 | tf_op jit(solution)/shard_map/ppermute | solution.py:63
  13.5 12.3 %collective-permute-start.2 = (f32[4,64,896]{2,1,0:T(8,128)}, f32[4,64,896]{2,1,0:T(8,128)}, u32[]{:S(2)}, u32[]{:S(2)}) collective-permute-start(f32[4,64,896]{2,1,0:T(8,128)} %get-tuple-element.21), channel_id=1, source_target_pairs={{0,32},{32,0},{1,33},{33,1},{2,34},{34,2},{3,35},{35,3},{4,36},{36... | collective-permute-start | bytes 2752520 | tf_op jit(solution)/shard_map/ppermute | solution.py:63
  14.0 18.7 %collective-permute-start.3 = (f32[4,64,896]{2,1,0:T(8,128)}, f32[4,64,896]{2,1,0:T(8,128)}, u32[]{:S(2)}, u32[]{:S(2)}) collective-permute-start(f32[4,64,896]{2,1,0:T(8,128)} %get-tuple-element.22), channel_id=1, source_target_pairs={{0,32},{32,0},{1,33},{33,1},{2,34},{34,2},{3,35},{35,3},{4,36},{36... | collective-permute-start | bytes 2752520 | tf_op jit(solution)/shard_map/ppermute | solution.py:63
  18.1 20.9 %collective-permute-start.5 = (f32[4,64,896]{2,1,0:T(8,128)}, f32[4,64,896]{2,1,0:T(8,128)S(1)}, u32[]{:S(2)}, u32[]{:S(2)}) collective-permute-start(f32[4,64,896]{2,1,0:T(8,128)} %get-tuple-element.24), channel_id=1, source_target_pairs={{0,32},{32,0},{1,33},{33,1},{2,34},{34,2},{3,35},{35,3},{4,36},{36... | collective-permute-start | bytes 2752520 | tf_op jit(solution)/shard_map/ppermute | solution.py:63
  19.3 1.0 copy-start.3
  19.3 19.8 %collective-permute-start.6 = (f32[4,64,896]{2,1,0:T(8,128)}, f32[4,64,896]{2,1,0:T(8,128)}, u32[]{:S(2)}, u32[]{:S(2)}) collective-permute-start(f32[4,64,896]{2,1,0:T(8,128)} %get-tuple-element.25), channel_id=1, source_target_pairs={{0,32},{32,0},{1,33},{33,1},{2,34},{34,2},{3,35},{35,3},{4,36},{36... | collective-permute-start | bytes 2752520 | tf_op jit(solution)/shard_map/ppermute | solution.py:63
  20.3 0.9 copy-start.5
  25.8 23.5 %collective-permute-start.9 = (f32[4,64,896]{2,1,0:T(8,128)}, f32[4,64,896]{2,1,0:T(8,128)}, u32[]{:S(2)}, u32[]{:S(2)}) collective-permute-start(f32[4,64,896]{2,1,0:T(8,128)} %get-tuple-element.29), channel_id=1, source_target_pairs={{0,64},{64,128},{128,192},{192,0},{1,65},{65,129},{129,193},{193,1... | collective-permute-start | bytes 2752520 | tf_op jit(solution)/shard_map/ppermute | solution.py:58
  25.8 26.0 %collective-permute-start.12 = (f32[4,64,896]{2,1,0:T(8,128)}, f32[4,64,896]{2,1,0:T(8,128)}, u32[]{:S(2)}, u32[]{:S(2)}) collective-permute-start(f32[4,64,896]{2,1,0:T(8,128)} %get-tuple-element.33), channel_id=1, source_target_pairs={{0,192},{64,0},{128,64},{192,128},{1,193},{65,1},{129,65},{193,129... | collective-permute-start | bytes 2752520 | tf_op jit(solution)/shard_map/ppermute | solution.py:58
  32.7 21.4 %collective-permute-start = (f32[4,64,896]{2,1,0:T(8,128)}, f32[4,64,896]{2,1,0:T(8,128)S(1)}, u32[]{:S(2)}, u32[]{:S(2)}) collective-permute-start(f32[4,64,896]{2,1,0:T(8,128)} %get-tuple-element.18), channel_id=1, source_target_pairs={{0,32},{32,0},{1,33},{33,1},{2,34},{34,2},{3,35},{35,3},{4,36},{36... | collective-permute-start | bytes 2752520 | tf_op jit(solution)/shard_map/ppermute | solution.py:63
  39.0 0.9 copy-start.2
  39.0 18.4 %collective-permute-start.1 = (f32[4,64,896]{2,1,0:T(8,128)}, f32[4,64,896]{2,1,0:T(8,128)S(1)}, u32[]{:S(2)}, u32[]{:S(2)}) collective-permute-start(f32[4,64,896]{2,1,0:T(8,128)} %get-tuple-element.19), channel_id=1, source_target_pairs={{0,32},{32,0},{1,33},{33,1},{2,34},{34,2},{3,35},{35,3},{4,36},{36... | collective-permute-start | bytes 2752520 | tf_op jit(solution)/shard_map/ppermute | solution.py:63
  39.1 28.8 %collective-permute-start.4 = (f32[4,64,896]{2,1,0:T(8,128)}, f32[4,64,896]{2,1,0:T(8,128)}, u32[]{:S(2)}, u32[]{:S(2)}) collective-permute-start(f32[4,64,896]{2,1,0:T(8,128)} %get-tuple-element.23), channel_id=1, source_target_pairs={{0,192},{64,0},{128,64},{192,128},{1,193},{65,1},{129,65},{193,129... | collective-permute-start | bytes 2752520 | tf_op jit(solution)/shard_map/ppermute | solution.py:58
  44.6 7.3 %copy-start.7 = (f32[4,64,896]{2,1,0:T(8,128)S(1)}, f32[4,64,896]{2,1,0:T(8,128)}, u32[]{:S(2)}) copy-start(f32[4,64,896]{2,1,0:T(8,128)} %get-tuple-element.32) | copy-start | bytes 2752516
  51.8 22.5 %collective-permute-start.10 = (f32[4,64,896]{2,1,0:T(8,128)}, f32[4,64,896]{2,1,0:T(8,128)S(1)}, u32[]{:S(2)}, u32[]{:S(2)}) collective-permute-start(f32[4,64,896]{2,1,0:T(8,128)} %add.114), channel_id=1, source_target_pairs={{0,64},{64,128},{128,192},{192,0},{1,65},{65,129},{129,193},{193,1... | collective-permute-start | bytes 2752520 | tf_op jit(solution)/shard_map/ppermute | solution.py:58
  51.9 42.3 %collective-permute-start.11 = (f32[4,64,896]{2,1,0:T(8,128)}, f32[4,64,896]{2,1,0:T(8,128)}, u32[]{:S(2)}, u32[]{:S(2)}) collective-permute-start(f32[4,64,896]{2,1,0:T(8,128)} %get-tuple-element.31), channel_id=1, source_target_pairs={{0,64},{64,128},{128,192},{192,0},{1,65},{65,129},{129,193},{193,1... | collective-permute-start | bytes 2752520 | tf_op jit(solution)/shard_map/ppermute | solution.py:58
  54.1 3.4 %copy-start.4 = (f32[4,64,896]{2,1,0:T(8,128)}, f32[4,64,896]{2,1,0:T(8,128)S(1)}, u32[]{:S(2)}) copy-start(f32[4,64,896]{2,1,0:T(8,128)S(1)} %collective-permute-done.other_first) | copy-start | bytes 2752516
  54.1 40.1 %collective-permute-start.13 = (f32[4,64,896]{2,1,0:T(8,128)}, f32[4,64,896]{2,1,0:T(8,128)}, u32[]{:S(2)}, u32[]{:S(2)}) collective-permute-start(f32[4,64,896]{2,1,0:T(8,128)} %add.117), channel_id=1, source_target_pairs={{0,192},{64,0},{128,64},{192,128},{1,193},{65,1},{129,65},{193,129... | collective-permute-start | bytes 2752520 | tf_op jit(solution)/shard_map/ppermute | solution.py:58
  57.4 1.0 copy-start.6
  246.5 2.2 copy-start.1
  246.7 3.5 %copy-start = (f32[4,2,8,8,896]{4,3,0,2,1:T(8,128)}, f32[4,2,8,8,896]{4,3,0,2,1:T(8,128)S(1)}, u32[]{:S(2)}) copy-start(f32[4,2,8,8,896]{4,3,0,2,1:T(8,128)S(1)} %copy.51) | copy-start | bytes 5505028

commit v2 on v0

v2 whole, which is shorter than its diff:
```python
import functools

import jax
import jax.numpy as jnp
from jax import lax
from jax.experimental import pallas as pl
from jax.experimental.pallas import tpu as pltpu
from jax.sharding import Mesh
from jax.sharding import PartitionSpec as P

DW = 4096
FW = 14336
ITERS = 5


EPSILON = 1e-06
LEARNING_RATE = 0.02
DECAY_RATE = 0.1
CORES = 2


def widen_kernel(steps, own, place, *refs):
    grads = refs[:steps]
    if own:
        other, outs = refs[steps], refs[steps + 1 :]
        for out in range(2 * steps):
            step, half = divmod(out, 2)
            outs[out][...] = grads[step][0, :, half].astype(jnp.float32) + other[step, half]
    else:
        for step in range(steps):
            for half in range(2):
                refs[-1][step, half] = grads[step][0, :, half].astype(jnp.float32)


def widen(grads, place, size, steps, other=None):
    _, groups, _, rows, columns = grads.shape
    width = columns // size
    deep = groups // 2
    own = other is not None

    def source(step):
        def index(j, place):
            matrix = place[1] if own else 1 - place[1]
            return (matrix, j, 0, 0, lax.rem(place[0] + step, size))

        return pl.BlockSpec((1, deep, 2, rows, width), index)

    flat = pl.BlockSpec((deep, rows, width), lambda j, place: (j, 0, 0))
    count = len(steps)
    joined = pl.BlockSpec((count, 2, deep, rows, width), lambda j, place: (0, 0, j, 0, 0))
    shape = (groups, rows, width)
    shapes = [shape] * (2 * count) if own else [(count, 2) + shape]
    return pl.pallas_call(
        functools.partial(widen_kernel, count, own),
        grid_spec=pltpu.PrefetchScalarGridSpec(
            num_scalar_prefetch=1,
            grid=(2,),
            in_specs=[source(step) for step in steps] + ([joined] if own else []),
            out_specs=[flat] * (2 * count) if own else [joined],
        ),
        out_shape=[jax.ShapeDtypeStruct(s, jnp.float32) for s in shapes],
        compiler_params=pltpu.CompilerParams(vmem_limit_bytes=40 * 2**20),
    )(place, *[grads] * count, *([other] if own else []))


def swap(values):
    return lax.ppermute(values, "core", [(0, 1), (1, 0)])


def move(values, size, step):
    return lax.ppermute(values, "x", [(i, (i + step) % size) for i in range(size)])


def after(values, earlier):
    return lax.optimization_barrier((values, earlier))[0]


def reduce_scatter(grads, place, size):
    def total(steps, place):
        other = swap(widen(grads, place, size, steps)[0])
        return widen(grads, place, size, steps, other)

    far_first, far_second = total((2,), place)
    right = move(far_first, size, 1)
    left = move(far_second, size, -1)
    next_first, next_second, last_first, last_second = total((1, 3), after(place, far_first))
    right_plain = move(next_second, size, 1)
    left_plain = move(last_first, size, -1)
    first, second = total((0,), after(place, far_first))
    next_first, last_second, right, left, first, second = lax.optimization_barrier(
        (next_first, last_second, right, left, first, second)
    )
    right_summed = move(next_first + right, size, 1)
    left_summed = move(last_second + left, size, -1)
    first = first + left_plain
    second = second + right_plain
    return first + right_summed, second + left_summed


def group_sum(part, axes, size):
    spread = jnp.broadcast_to(part[None, None, :], (size, 1) + part.shape)
    return jnp.sum(lax.all_to_all(spread, axes, 0, 0, tiled=True), axis=(0, 1))


def per_device(sizes, grad_parts, weights):
    size_x, size_row, size_col = sizes
    _, _, blocks, rows, columns = grad_parts.shape
    x = lax.axis_index("x")
    core = lax.axis_index("core")
    place = jnp.stack([x, core]).astype(jnp.int32)
    grads = grad_parts.reshape(2, size_x, CORES, rows, columns)
    halves = reduce_scatter(grads, place, size_x)
    width = columns // size_x

    values = [h.reshape(size_x * rows, width) for h in halves]
    row_factor = jnp.ones((CORES, size_x * rows), jnp.float32)
    column_factor = jnp.ones((width,), jnp.float32)

    def scaled():
        return [
            v * r[:, None] * column_factor[None, :] for v, r in zip(values, row_factor)
        ]

    for sweep in range(ITERS):
        part = jnp.concatenate([jnp.sum(v * v, axis=1) for v in scaled()])
        total = group_sum(part, ("x", "col"), size_x * size_col)
        row_factor = row_factor * lax.rsqrt(total / FW + EPSILON).reshape(CORES, -1)
        part = sum(jnp.sum(v * v, axis=0) for v in scaled())
        total = group_sum(part, ("row",), size_row)
        column_factor = column_factor * lax.rsqrt(total / DW + EPSILON)

    direction = jnp.stack([v.reshape(size_x, rows, width) for v in scaled()], axis=1)
    direction = direction.reshape(blocks, rows, width)
    direction = lax.all_to_all(direction, ("x", "core"), 0, 0, tiled=True)
    direction = direction.reshape(size_x, CORES, rows, width).transpose(1, 2, 0, 3)
    direction = direction.reshape(CORES, rows, columns)
    updated = weights * (1.0 - LEARNING_RATE * DECAY_RATE) - LEARNING_RATE * direction
    return (updated, direction)


def solution(mesh):
    size_x = mesh.shape["rep"] // CORES
    sizes = (size_x, mesh.shape["row"], mesh.shape["col"])
    split = Mesh(
        mesh.devices.reshape((size_x, CORES) + sizes[1:]), ("x", "core", "row", "col")
    )
    rep = ("x", "core")
    in_specs = (P(rep, None, None, "row", "col"), P(None, rep + ("row",), "col"))
    out_specs = (P(None, rep + ("row",), "col"), P(None, rep + ("row",), "col"))

    def run(grad_parts, weights):
        return per_device(sizes, grad_parts, weights)

    return jax.shard_map(
        run, mesh=split, in_specs=in_specs, out_specs=out_specs, check_vma=False
    )
```

time: 1420 us -> 235 us (0.17)
  blocking collectives: 1270 us -> 140 us
  waiting for transfers between devices: 104 us -> 57.3 us
    psum x10 -> x0, blocking collectives: 1270 us -> none  [the longest x5 1230 us: normalize(): column_total = lax.psum(column_part, ('rep', 'row'))]
    all_to_all x0 -> x11, blocking collectives: none -> 140 us  [the longest x10 97.8 us: group_sum(): return jnp.sum(lax.all_to_all(spread, axes, 0, 0, tiled=True), axis=(0, 1))]
    reduce_scatter x2 -> x0, waiting for transfers between devices: 103 us -> none  [per_device(): lax.psum_scatter(grad_parts[0, matrix].astype(jnp.float32), 'rep', scatte...]
    ppermute x0 -> x9, waiting for transfers between devices: none -> 57.3 us  [the longest x6 49 us: move(): lax.ppermute(values, 'x', [(i, (i + step) % size) for i in range(size)])]
  transfers between devices with their start and end apart: 2 -> 9, of which waited for: 2 -> 6; matrix products, arithmetic and copies ran while one was open for 0% -> 1% of each run, Pallas kernels for 0% -> 2%
where the time goes in v2:
time: 235 us; the launch traced here: 234 us
  blocking collectives  140 us (60%)
  waiting for transfers between devices  57.3 us (24%)
  starting transfers between devices  11.9 us (5%)
  other arithmetic  9.86 us (4%)
  Pallas kernels  7.36 us (3%)
  local copies, waits for them, and re-layouts  7.25 us (3%)
    all_to_all x10, blocking collectives, group_sum(): return jnp.sum(lax.all_to_all(spread, axes, 0, 0, tiled=True), axis=(0, 1))  97.8 us
    ppermute x6, waiting for transfers between devices, move(): lax.ppermute(values, 'x', [(i, (i + step) % size) for i in range(size)])  49 us
    all_to_all x1, blocking collectives, per_device(): direction = lax.all_to_all(direction, ('x', 'core'), 0, 0, tiled=True)  41.7 us
    ppermute x3, waiting for transfers between devices, swap(): return lax.ppermute(values, 'core', [(0, 1), (1, 0)])  8.22 us
    ppermute x6, starting transfers between devices, move(): lax.ppermute(values, 'x', [(i, (i + step) % size) for i in range(size)])  7.89 us
    pallas_call x6, Pallas kernels, widen(): pl.pallas_call(functools.partial(widen_kernel, count, own), grid_spec=plt...  7.36 us
    unnamed x6, local copies, waits for them, and re-layouts  5.03 us
  transfers between devices with their start and end apart: 9, of which 6 were waited for; matrix products, arithmetic and copies ran while one was open for 1% of the time, Pallas kernels for 2%

profile of v2, /device:TPU:1, one launch (start us, length us, event | category | flops | bytes accessed | tf_op | source)
XLA Modules:
  0.0 234.1 jit_solution(1890105470567615620)
XLA Ops:
  0.7 3.1 %copy-done = bf16[1,2,8,64,3584]{4,3,2,1,0:T(8,128)(2,1)S(1)} copy-done((bf16[1,2,8,64,3584]{4,3,2,1,0:T(8,128)(2,1)S(1)}, bf16[1,2,8,64,3584]{4,3,2,1,0:T(8,128)(2,1)}, u32[]{:S(2)}) %copy-start) | copy-done | bytes 7340056
  3.8 0.9 shard_map.41
  4.7 3.3 %collective-permute-start = (f32[1,2,4,64,896]{4,3,2,1,0:T(8,128)S(1)}, f32[1,2,4,64,896]{4,3,2,1,0:T(8,128)S(1)}, u32[]{:S(2)}, u32[]{:S(2)}) collective-permute-start(f32[1,2,4,64,896]{4,3,2,1,0:T(8,128)S(1)} %shard_map.41), channel_id=1, source_target_pairs={{0,32},{32,0},{1,33},{33,1},{2,34},{34,2},{3,35},{35,3},{4,36},{36... | collective-permute-start | bytes 5505032 | tf_op jit(solution)/shard_map/ppermute | solution.py:67
  8.1 3.4 %collective-permute-done.refs_1_ = f32[1,2,4,64,896]{4,3,2,1,0:T(8,128)S(1)} collective-permute-done((f32[1,2,4,64,896]{4,3,2,1,0:T(8,128)S(1)}, f32[1,2,4,64,896]{4,3,2,1,0:T(8,128)S(1)}, u32[]{:S(2)}, u32[]{:S(2)}) %collective-permute-start) | collective-permute-done | bytes 1835040 | tf_op jit(solution)/shard_map/ppermute | solution.py:67
  11.5 1.0 shard_map.42
  12.5 1.3 shard_map.43
  15.4 2.7 %collective-permute-start.3 = (f32[4,64,896]{2,1,0:T(8,128)S(1)}, f32[4,64,896]{2,1,0:T(8,128)}, u32[]{:S(2)}, u32[]{:S(2)}) collective-permute-start(f32[4,64,896]{2,1,0:T(8,128)S(1)} %get-tuple-element.21), channel_id=1, source_target_pairs={{0,192},{64,0},{128,64},{192,128},{1,193},{65,1},{129,65},{193,129... | collective-permute-start | bytes 2752520 | tf_op jit(solution)/shard_map/ppermute | solution.py:71
  18.1 4.8 %collective-permute-done.4.refs_1_ = f32[1,2,4,64,896]{4,3,2,1,0:T(8,128)S(1)} collective-permute-done((f32[1,2,4,64,896]{4,3,2,1,0:T(8,128)S(1)}, f32[1,2,4,64,896]{4,3,2,1,0:T(8,128)S(1)}, u32[]{:S(2)}, u32[]{:S(2)}) %collective-permute-start.4) | collective-permute-done | bytes 1835040 | tf_op jit(solution)/shard_map/ppermute | solution.py:67
  22.9 1.0 shard_map.46
  23.9 2.2 shard_map.44
  26.1 12.1 %collective-permute-done.2 = f32[4,64,896]{2,1,0:T(8,128)S(1)} collective-permute-done((f32[4,64,896]{2,1,0:T(8,128)S(1)}, f32[4,64,896]{2,1,0:T(8,128)S(1)}, u32[]{:S(2)}, u32[]{:S(2)}) %collective-permute-start.2) | collective-permute-done | bytes 917536 | tf_op jit(solution)/shard_map/ppermute | solution.py:71
  38.2 1.3 add.150
  39.5 2.5 %collective-permute-start.8 = (f32[4,64,896]{2,1,0:T(8,128)S(1)}, f32[4,64,896]{2,1,0:T(8,128)S(1)}, u32[]{:S(2)}, u32[]{:S(2)}) collective-permute-start(f32[4,64,896]{2,1,0:T(8,128)S(1)} %add.150), channel_id=1, source_target_pairs={{0,192},{64,0},{128,64},{192,128},{1,193},{65,1},{129,65},{193,129... | collective-permute-start | bytes 2752520 | tf_op jit(solution)/shard_map/ppermute | solution.py:71
  42.0 1.1 add.147
  43.1 2.7 %collective-permute-start.5 = (f32[4,64,896]{2,1,0:T(8,128)S(1)}, f32[4,64,896]{2,1,0:T(8,128)}, u32[]{:S(2)}, u32[]{:S(2)}) collective-permute-start(f32[4,64,896]{2,1,0:T(8,128)S(1)} %get-tuple-element.25), channel_id=1, source_target_pairs={{0,192},{64,0},{128,64},{192,128},{1,193},{65,1},{129,65},{193,129... | collective-permute-start | bytes 2752520 | tf_op jit(solution)/shard_map/ppermute | solution.py:71
  45.8 14.4 %collective-permute-done.8 = f32[4,64,896]{2,1,0:T(8,128)S(1)} collective-permute-done((f32[4,64,896]{2,1,0:T(8,128)S(1)}, f32[4,64,896]{2,1,0:T(8,128)S(1)}, u32[]{:S(2)}, u32[]{:S(2)}) %collective-permute-start.8) | collective-permute-done | bytes 917536 | tf_op jit(solution)/shard_map/ppermute | solution.py:71
  60.2 3.1 %collective-permute-done.7 = f32[4,64,896]{2,1,0:T(8,128)S(1)} collective-permute-done((f32[4,64,896]{2,1,0:T(8,128)S(1)}, f32[4,64,896]{2,1,0:T(8,128)S(1)}, u32[]{:S(2)}, u32[]{:S(2)}) %collective-permute-start.7) | collective-permute-done | bytes 917536 | tf_op jit(solution)/shard_map/ppermute | solution.py:71
  63.6 19.5 %collective-permute-done.6 = f32[4,64,896]{2,1,0:T(8,128)} collective-permute-done((f32[4,64,896]{2,1,0:T(8,128)}, f32[4,64,896]{2,1,0:T(8,128)}, u32[]{:S(2)}, u32[]{:S(2)}) %collective-permute-start.6) | collective-permute-done | bytes 917536 | tf_op jit(solution)/shard_map/ppermute | solution.py:71
  83.0 1.7 multiply_reduce_fusion.19
  84.8 9.0 %all_to_all.55 = f32[16,1,512]{2,1,0:T(1,128)S(1)} all-to-all(f32[16,1,512]{2,1,0:T(1,128)S(1)} %broadcast_in_dim.20), channel_id=1, replica_groups=mesh['x'=4,'core'=2,'row'=8,'col'=4] {'x','col'}, dimensions={0} | all-to-all | bytes 65536 | tf_op jit(solution)/shard_map/all_to_all | solution.py:102
  94.4 14.6 %all_to_all.56 = f32[8,1,896]{2,1,0:T(1,128)S(1)} all-to-all(f32[8,1,896]{2,1,0:T(1,128)S(1)} %broadcast_in_dim.21), channel_id=1, replica_groups=mesh['x'=4,'core'=2,'row'=8,'col'=4] {'row'}, dimensions={0} | all-to-all | bytes 57344 | tf_op jit(solution)/shard_map/all_to_all | solution.py:102
  109.7 9.3 %all_to_all.57 = f32[16,1,512]{2,1,0:T(1,128)S(1)} all-to-all(f32[16,1,512]{2,1,0:T(1,128)S(1)} %broadcast_in_dim.22), channel_id=1, replica_groups=mesh['x'=4,'core'=2,'row'=8,'col'=4] {'x','col'}, dimensions={0} | all-to-all | bytes 65536 | tf_op jit(solution)/shard_map/all_to_all | solution.py:102
  119.5 9.2 %all_to_all.58 = f32[8,1,896]{2,1,0:T(1,128)S(1)} all-to-all(f32[8,1,896]{2,1,0:T(1,128)S(1)} %broadcast_in_dim.23), channel_id=1, replica_groups=mesh['x'=4,'core'=2,'row'=8,'col'=4] {'row'}, dimensions={0} | all-to-all | bytes 57344 | tf_op jit(solution)/shard_map/all_to_all | solution.py:102
  129.4 9.3 %all_to_all.59 = f32[16,1,512]{2,1,0:T(1,128)S(1)} all-to-all(f32[16,1,512]{2,1,0:T(1,128)S(1)} %broadcast_in_dim.24), channel_id=1, replica_groups=mesh['x'=4,'core'=2,'row'=8,'col'=4] {'x','col'}, dimensions={0} | all-to-all | bytes 65536 | tf_op jit(solution)/shard_map/all_to_all | solution.py:102
  139.3 9.2 %all_to_all.60 = f32[8,1,896]{2,1,0:T(1,128)S(1)} all-to-all(f32[8,1,896]{2,1,0:T(1,128)S(1)} %broadcast_in_dim.25), channel_id=1, replica_groups=mesh['x'=4,'core'=2,'row'=8,'col'=4] {'row'}, dimensions={0} | all-to-all | bytes 57344 | tf_op jit(solution)/shard_map/all_to_all | solution.py:102
  149.1 9.3 %all_to_all.61 = f32[16,1,512]{2,1,0:T(1,128)S(1)} all-to-all(f32[16,1,512]{2,1,0:T(1,128)S(1)} %broadcast_in_dim.26), channel_id=1, replica_groups=mesh['x'=4,'core'=2,'row'=8,'col'=4] {'x','col'}, dimensions={0} | all-to-all | bytes 65536 | tf_op jit(solution)/shard_map/all_to_all | solution.py:102
  159.0 9.2 %all_to_all.62 = f32[8,1,896]{2,1,0:T(1,128)S(1)} all-to-all(f32[8,1,896]{2,1,0:T(1,128)S(1)} %broadcast_in_dim.27), channel_id=1, replica_groups=mesh['x'=4,'core'=2,'row'=8,'col'=4] {'row'}, dimensions={0} | all-to-all | bytes 57344 | tf_op jit(solution)/shard_map/all_to_all | solution.py:102
  168.8 9.6 %all_to_all.63 = f32[16,1,512]{2,1,0:T(1,128)S(1)} all-to-all(f32[16,1,512]{2,1,0:T(1,128)S(1)} %broadcast_in_dim.28), channel_id=1, replica_groups=mesh['x'=4,'core'=2,'row'=8,'col'=4] {'x','col'}, dimensions={0} | all-to-all | bytes 65536 | tf_op jit(solution)/shard_map/all_to_all | solution.py:102
  179.0 9.2 %all_to_all.64 = f32[8,1,896]{2,1,0:T(1,128)S(1)} all-to-all(f32[8,1,896]{2,1,0:T(1,128)S(1)} %broadcast_in_dim.29), channel_id=1, replica_groups=mesh['x'=4,'core'=2,'row'=8,'col'=4] {'row'}, dimensions={0} | all-to-all | bytes 57344 | tf_op jit(solution)/shard_map/all_to_all | solution.py:102
  188.7 41.7 %all_to_all.65 = f32[8,64,896]{2,1,0:T(8,128)S(1)} all-to-all(f32[8,64,896]{2,1,0:T(8,128)S(1)} %bitcast.21), channel_id=1, replica_groups=mesh['x'=4,'core'=2,'row'=8,'col'=4] {'x','core'}, dimensions={0} | all-to-all | bytes 3670016 | tf_op jit(solution)/shard_map/all_to_all | solution.py:134
  230.6 1.9 copy-done.2
  232.6 1.5 multiply_subtract_fusion
  (93 shorter events, 8.2 us)
Async XLA Ops:
  0.7 3.1 %copy-start = (bf16[1,2,8,64,3584]{4,3,2,1,0:T(8,128)(2,1)S(1)}, bf16[1,2,8,64,3584]{4,3,2,1,0:T(8,128)(2,1)}, u32[]{:S(2)}) copy-start(bf16[1,2,8,64,3584]{4,3,2,1,0:T(8,128)(2,1)} %param.2) | copy-start | bytes 22020100
  4.7 6.7 %collective-permute-start = (f32[1,2,4,64,896]{4,3,2,1,0:T(8,128)S(1)}, f32[1,2,4,64,896]{4,3,2,1,0:T(8,128)S(1)}, u32[]{:S(2)}, u32[]{:S(2)}) collective-permute-start(f32[1,2,4,64,896]{4,3,2,1,0:T(8,128)S(1)} %shard_map.41), channel_id=1, source_target_pairs={{0,32},{32,0},{1,33},{33,1},{2,34},{34,2},{3,35},{35,3},{4,36},{36... | collective-permute-start | bytes 5505032 | tf_op jit(solution)/shard_map/ppermute | solution.py:67
  13.8 10.1 %collective-permute-start.1 = (f32[2,2,4,64,896]{4,3,2,1,0:T(8,128)S(1)}, f32[2,2,4,64,896]{4,3,2,1,0:T(8,128)S(1)}, u32[]{:S(2)}, u32[]{:S(2)}) collective-permute-start(f32[2,2,4,64,896]{4,3,2,1,0:T(8,128)S(1)} %shard_map.43), channel_id=1, source_target_pairs={{0,32},{32,0},{1,33},{33,1},{2,34},{34,2},{3,35},{35,3},{4,36},{36... | collective-permute-start | bytes 11010056 | tf_op jit(solution)/shard_map/ppermute | solution.py:67
  15.2 7.7 %collective-permute-start.4 = (f32[1,2,4,64,896]{4,3,2,1,0:T(8,128)S(1)}, f32[1,2,4,64,896]{4,3,2,1,0:T(8,128)S(1)}, u32[]{:S(2)}, u32[]{:S(2)}) collective-permute-start(f32[1,2,4,64,896]{4,3,2,1,0:T(8,128)S(1)} %shard_map.45), channel_id=1, source_target_pairs={{0,32},{32,0},{1,33},{33,1},{2,34},{34,2},{3,35},{35,3},{4,36},{36... | collective-permute-start | bytes 5505032 | tf_op jit(solution)/shard_map/ppermute | solution.py:67
  15.4 22.8 %collective-permute-start.2 = (f32[4,64,896]{2,1,0:T(8,128)S(1)}, f32[4,64,896]{2,1,0:T(8,128)S(1)}, u32[]{:S(2)}, u32[]{:S(2)}) collective-permute-start(f32[4,64,896]{2,1,0:T(8,128)S(1)} %get-tuple-element.17), channel_id=1, source_target_pairs={{0,64},{64,128},{128,192},{192,0},{1,65},{65,129},{129,193},{193,1... | collective-permute-start | bytes 2752520 | tf_op jit(solution)/shard_map/ppermute | solution.py:71
  15.4 22.8 %collective-permute-start.3 = (f32[4,64,896]{2,1,0:T(8,128)S(1)}, f32[4,64,896]{2,1,0:T(8,128)}, u32[]{:S(2)}, u32[]{:S(2)}) collective-permute-start(f32[4,64,896]{2,1,0:T(8,128)S(1)} %get-tuple-element.21), channel_id=1, source_target_pairs={{0,192},{64,0},{128,64},{192,128},{1,193},{65,1},{129,65},{193,129... | collective-permute-start | bytes 2752520 | tf_op jit(solution)/shard_map/ppermute | solution.py:71
  39.5 20.7 %collective-permute-start.8 = (f32[4,64,896]{2,1,0:T(8,128)S(1)}, f32[4,64,896]{2,1,0:T(8,128)S(1)}, u32[]{:S(2)}, u32[]{:S(2)}) collective-permute-start(f32[4,64,896]{2,1,0:T(8,128)S(1)} %add.150), channel_id=1, source_target_pairs={{0,192},{64,0},{128,64},{192,128},{1,193},{65,1},{129,65},{193,129... | collective-permute-start | bytes 2752520 | tf_op jit(solution)/shard_map/ppermute | solution.py:71
  42.0 21.2 %collective-permute-start.7 = (f32[4,64,896]{2,1,0:T(8,128)S(1)}, f32[4,64,896]{2,1,0:T(8,128)S(1)}, u32[]{:S(2)}, u32[]{:S(2)}) collective-permute-start(f32[4,64,896]{2,1,0:T(8,128)S(1)} %get-tuple-element.29), channel_id=1, source_target_pairs={{0,64},{64,128},{128,192},{192,0},{1,65},{65,129},{129,193},{193,1... | collective-permute-start | bytes 2752520 | tf_op jit(solution)/shard_map/ppermute | solution.py:71
  43.1 40.0 %collective-permute-start.6 = (f32[4,64,896]{2,1,0:T(8,128)}, f32[4,64,896]{2,1,0:T(8,128)}, u32[]{:S(2)}, u32[]{:S(2)}) collective-permute-start(f32[4,64,896]{2,1,0:T(8,128)} %add.147), channel_id=1, source_target_pairs={{0,64},{64,128},{128,192},{192,0},{1,65},{65,129},{129,193},{193,1... | collective-permute-start | bytes 2752520 | tf_op jit(solution)/shard_map/ppermute | solution.py:71
  43.1 40.0 %collective-permute-start.5 = (f32[4,64,896]{2,1,0:T(8,128)S(1)}, f32[4,64,896]{2,1,0:T(8,128)}, u32[]{:S(2)}, u32[]{:S(2)}) collective-permute-start(f32[4,64,896]{2,1,0:T(8,128)S(1)} %get-tuple-element.25), channel_id=1, source_target_pairs={{0,192},{64,0},{128,64},{192,128},{1,193},{65,1},{129,65},{193,129... | collective-permute-start | bytes 2752520 | tf_op jit(solution)/shard_map/ppermute | solution.py:71
  230.4 2.2 copy-start.2
  230.6 3.5 %copy-start.1 = (f32[4,2,8,8,896]{4,3,0,2,1:T(8,128)}, f32[4,2,8,8,896]{4,3,0,2,1:T(8,128)S(1)}, u32[]{:S(2)}) copy-start(f32[4,2,8,8,896]{4,3,0,2,1:T(8,128)S(1)} %copy.31) | copy-start | bytes 5505028

commit v3 on v2

--- a/solution.py
+++ b/solution.py
@@ -83,13 +83,10 @@
     far_first, far_second = total((2,), place)
     right = move(far_first, size, 1)
     left = move(far_second, size, -1)
-    next_first, next_second, last_first, last_second = total((1, 3), after(place, far_first))
+    parts = total((1, 3, 0), after(place, far_first))
+    next_first, next_second, last_first, last_second, first, second = parts
     right_plain = move(next_second, size, 1)
     left_plain = move(last_first, size, -1)
-    first, second = total((0,), after(place, far_first))
-    next_first, last_second, right, left, first, second = lax.optimization_barrier(
-        (next_first, last_second, right, left, first, second)
-    )
     right_summed = move(next_first + right, size, 1)
     left_summed = move(last_second + left, size, -1)
     first = first + left_plain
@@ -100,6 +97,25 @@
 def group_sum(part, axes, size):
     spread = jnp.broadcast_to(part[None, None, :], (size, 1) + part.shape)
     return jnp.sum(lax.all_to_all(spread, axes, 0, 0, tiled=True), axis=(0, 1))
+
+
+def update_kernel(pieces, weights, updated, direction):
+    values = pieces[...]
+    direction[...] = values
+    updated[...] = weights[...] * (1.0 - LEARNING_RATE * DECAY_RATE) - LEARNING_RATE * values
+
+
+def update(pieces, weights):
+    _, rows, width = pieces.shape
+    side = pl.BlockSpec((CORES, rows, width), lambda i: (0, 0, i))
+    return pl.pallas_call(
+        update_kernel,
+        grid=(pieces.shape[0] // CORES,),
+        in_specs=[pl.BlockSpec((CORES, rows, width), lambda i: (i, 0, 0)), side],
+        out_specs=[side, side],
+        out_shape=[jax.ShapeDtypeStruct(weights.shape, jnp.float32)] * 2,
+        compiler_params=pltpu.CompilerParams(vmem_limit_bytes=40 * 2**20),
+    )(pieces, weights)
 
 
 def per_device(sizes, grad_parts, weights):
@@ -132,10 +148,7 @@
     direction = jnp.stack([v.reshape(size_x, rows, width) for v in scaled()], axis=1)
     direction = direction.reshape(blocks, rows, width)
     direction = lax.all_to_all(direction, ("x", "core"), 0, 0, tiled=True)
-    direction = direction.reshape(size_x, CORES, rows, width).transpose(1, 2, 0, 3)
-    direction = direction.reshape(CORES, rows, columns)
-    updated = weights * (1.0 - LEARNING_RATE * DECAY_RATE) - LEARNING_RATE * direction
-    return (updated, direction)
+    return update(direction, weights)
 
 
 def solution(mesh):

time: 235 us -> 229 us (0.974)
  other arithmetic: 9.86 us -> 7.21 us
    pallas_call x0 -> x1, Pallas kernels: none -> 2.39 us  [update(): pl.pallas_call(update_kernel, grid=(pieces.shape[0] // CORES,), in_specs=...]
    unnamed x6 -> x4, local copies, waits for them, and re-layouts: 5.03 us -> 3.09 us
    pallas_call x6 -> x4, Pallas kernels: 7.36 us -> 6.16 us  [widen(): pl.pallas_call(functools.partial(widen_kernel, count, own), grid_spec=plt...]
    ppermute x3 -> x2, waiting for transfers between devices: 8.22 us -> 9.39 us  [swap(): return lax.ppermute(values, 'core', [(0, 1), (1, 0)])]
  transfers between devices with their start and end apart: 9 -> 8, of which waited for: 6 -> 6; matrix products, arithmetic and copies ran while one was open for 1% -> 1% of each run, Pallas kernels for 2% -> 1%
where the time goes in v3:
time: 229 us
  blocking collectives  139 us (61%)
  waiting for transfers between devices  58.1 us (25%)
  starting transfers between devices  10.1 us (4%)
  Pallas kernels  8.55 us (4%)
  other arithmetic  7.21 us (3%)
  local copies, waits for them, and re-layouts  5.09 us (2%)
    all_to_all x10, blocking collectives, group_sum(): return jnp.sum(lax.all_to_all(spread, axes, 0, 0, tiled=True), axis=(0, 1))  98 us
    ppermute x6, waiting for transfers between devices, move(): lax.ppermute(values, 'x', [(i, (i + step) % size) for i in range(size)])  48.7 us
    all_to_all x1, blocking collectives, per_device(): direction = lax.all_to_all(direction, ('x', 'core'), 0, 0, tiled=True)  40.8 us
    ppermute x2, waiting for transfers between devices, swap(): return lax.ppermute(values, 'core', [(0, 1), (1, 0)])  9.39 us
    ppermute x6, starting transfers between devices, move(): lax.ppermute(values, 'x', [(i, (i + step) % size) for i in range(size)])  6.32 us
    pallas_call x4, Pallas kernels, widen(): pl.pallas_call(functools.partial(widen_kernel, count, own), grid_spec=plt...  6.16 us
  transfers between devices with their start and end apart: 8, of which 6 were waited for; matrix products, arithmetic and copies ran while one was open for 1% of the time, Pallas kernels for 1%

profile of v3, /device:TPU:1, one launch (start us, length us, event | category | flops | bytes accessed | tf_op | source)
XLA Modules:
  0.0 228.8 jit_solution(11370088243436414869)
XLA Ops:
  0.7 3.1 %copy-done = bf16[1,2,8,64,3584]{4,3,2,1,0:T(8,128)(2,1)S(1)} copy-done((bf16[1,2,8,64,3584]{4,3,2,1,0:T(8,128)(2,1)S(1)}, bf16[1,2,8,64,3584]{4,3,2,1,0:T(8,128)(2,1)}, u32[]{:S(2)}) %copy-start) | copy-done | bytes 7340056
  3.8 0.9 shard_map.41
  4.7 3.3 %collective-permute-start = (f32[1,2,4,64,896]{4,3,2,1,0:T(8,128)S(1)}, f32[1,2,4,64,896]{4,3,2,1,0:T(8,128)S(1)}, u32[]{:S(2)}, u32[]{:S(2)}) collective-permute-start(f32[1,2,4,64,896]{4,3,2,1,0:T(8,128)S(1)} %shard_map.41), channel_id=1, source_target_pairs={{0,32},{32,0},{1,33},{33,1},{2,34},{34,2},{3,35},{35,3},{4,36},{36... | collective-permute-start | bytes 5505032 | tf_op jit(solution)/shard_map/ppermute | solution.py:67
  8.1 3.4 %collective-permute-done.refs_1_ = f32[1,2,4,64,896]{4,3,2,1,0:T(8,128)S(1)} collective-permute-done((f32[1,2,4,64,896]{4,3,2,1,0:T(8,128)S(1)}, f32[1,2,4,64,896]{4,3,2,1,0:T(8,128)S(1)}, u32[]{:S(2)}, u32[]{:S(2)}) %collective-permute-start) | collective-permute-done | bytes 1835040 | tf_op jit(solution)/shard_map/ppermute | solution.py:67
  11.5 1.0 shard_map.42
  12.5 1.6 shard_map.43
  14.1 0.5 collective-permute-start.1
  14.6 2.7 %collective-permute-start.6 = (f32[4,64,896]{2,1,0:T(8,128)S(1)}, f32[4,64,896]{2,1,0:T(8,128)S(1)}, u32[]{:S(2)}, u32[]{:S(2)}) collective-permute-start(f32[4,64,896]{2,1,0:T(8,128)S(1)} %get-tuple-element.19), channel_id=1, source_target_pairs={{0,192},{64,0},{128,64},{192,128},{1,193},{65,1},{129,65},{193,129... | collective-permute-start | bytes 2752520 | tf_op jit(solution)/shard_map/ppermute | solution.py:71
  17.2 6.0 %collective-permute-done.1.refs_3_ = f32[3,2,4,64,896]{4,3,2,1,0:T(8,128)S(1)} collective-permute-done((f32[3,2,4,64,896]{4,3,2,1,0:T(8,128)S(1)}, f32[3,2,4,64,896]{4,3,2,1,0:T(8,128)S(1)}, u32[]{:S(2)}, u32[]{:S(2)}) %collective-permute-start.1) | collective-permute-done | bytes 5505056 | tf_op jit(solution)/shard_map/ppermute | solution.py:67
  23.2 2.6 %shard_map.44 = (f32[4,64,896]{2,1,0:T(8,128)S(1)}, f32[4,64,896]{2,1,0:T(8,128)S(1)}, f32[4,64,896]{2,1,0:T(8,128)S(1)}, f32[4,64,896]{2,1,0:T(8,128)S(1)}, f32...) custom-call(s32[2]{0:T(128)S(1)} %pad_add_fusion.place, bf16[2,4,2,64,3584]{4,3,2,1,0:T(8,128)(2,1)} %bitcast.8, ...), custom_call_target="tpu_custom_call" | custom-call | tf_op jit(solution)/shard_map/pallas_call | solution.py:53
  25.8 0.8 collective-permute-start.2
  26.7 10.9 %collective-permute-done.3 = f32[4,64,896]{2,1,0:T(8,128)S(1)} collective-permute-done((f32[4,64,896]{2,1,0:T(8,128)S(1)}, f32[4,64,896]{2,1,0:T(8,128)S(1)}, u32[]{:S(2)}, u32[]{:S(2)}) %collective-permute-start.3) | collective-permute-done | bytes 917536 | tf_op jit(solution)/shard_map/ppermute | solution.py:71
  37.9 1.1 add.150
  39.0 2.7 %collective-permute-start.7 = (f32[4,64,896]{2,1,0:T(8,128)}, f32[4,64,896]{2,1,0:T(8,128)}, u32[]{:S(2)}, u32[]{:S(2)}) collective-permute-start(f32[4,64,896]{2,1,0:T(8,128)} %add.150), channel_id=1, source_target_pairs={{0,192},{64,0},{128,64},{192,128},{1,193},{65,1},{129,65},{193,129... | collective-permute-start | bytes 2752520 | tf_op jit(solution)/shard_map/ppermute | solution.py:71
  41.6 14.6 %collective-permute-done.2 = f32[4,64,896]{2,1,0:T(8,128)S(1)} collective-permute-done((f32[4,64,896]{2,1,0:T(8,128)S(1)}, f32[4,64,896]{2,1,0:T(8,128)S(1)}, u32[]{:S(2)}, u32[]{:S(2)}) %collective-permute-start.2) | collective-permute-done | bytes 917536 | tf_op jit(solution)/shard_map/ppermute | solution.py:71
  56.2 3.7 %collective-permute-done.4 = f32[4,64,896]{2,1,0:T(8,128)S(1)} collective-permute-done((f32[4,64,896]{2,1,0:T(8,128)S(1)}, f32[4,64,896]{2,1,0:T(8,128)S(1)}, u32[]{:S(2)}, u32[]{:S(2)}) %collective-permute-start.4) | collective-permute-done | bytes 917536 | tf_op jit(solution)/shard_map/ppermute | solution.py:71
  60.2 19.5 %collective-permute-done.5 = f32[4,64,896]{2,1,0:T(8,128)} collective-permute-done((f32[4,64,896]{2,1,0:T(8,128)S(1)}, f32[4,64,896]{2,1,0:T(8,128)}, u32[]{:S(2)}, u32[]{:S(2)}) %collective-permute-start.5) | collective-permute-done | bytes 917536 | tf_op jit(solution)/shard_map/ppermute | solution.py:71
  79.7 1.7 multiply_reduce_fusion.18
  81.5 9.0 %all_to_all.55 = f32[16,1,512]{2,1,0:T(1,128)S(1)} all-to-all(f32[16,1,512]{2,1,0:T(1,128)S(1)} %broadcast_in_dim.20), channel_id=1, replica_groups=mesh['x'=4,'core'=2,'row'=8,'col'=4] {'x','col'}, dimensions={0} | all-to-all | bytes 65536 | tf_op jit(solution)/shard_map/all_to_all | solution.py:99
  91.0 14.7 %all_to_all.56 = f32[8,1,896]{2,1,0:T(1,128)S(1)} all-to-all(f32[8,1,896]{2,1,0:T(1,128)S(1)} %broadcast_in_dim.21), channel_id=1, replica_groups=mesh['x'=4,'core'=2,'row'=8,'col'=4] {'row'}, dimensions={0} | all-to-all | bytes 57344 | tf_op jit(solution)/shard_map/all_to_all | solution.py:99
  105.8 0.4 multiply_reduce_fusion.15
  106.4 9.6 %all_to_all.57 = f32[16,1,512]{2,1,0:T(1,128)S(1)} all-to-all(f32[16,1,512]{2,1,0:T(1,128)S(1)} %broadcast_in_dim.22), channel_id=1, replica_groups=mesh['x'=4,'core'=2,'row'=8,'col'=4] {'x','col'}, dimensions={0} | all-to-all | bytes 65536 | tf_op jit(solution)/shard_map/all_to_all | solution.py:99
  116.5 9.2 %all_to_all.58 = f32[8,1,896]{2,1,0:T(1,128)S(1)} all-to-all(f32[8,1,896]{2,1,0:T(1,128)S(1)} %broadcast_in_dim.23), channel_id=1, replica_groups=mesh['x'=4,'core'=2,'row'=8,'col'=4] {'row'}, dimensions={0} | all-to-all | bytes 57344 | tf_op jit(solution)/shard_map/all_to_all | solution.py:99
  125.8 0.4 multiply_reduce_fusion.11
  126.4 9.3 %all_to_all.59 = f32[16,1,512]{2,1,0:T(1,128)S(1)} all-to-all(f32[16,1,512]{2,1,0:T(1,128)S(1)} %broadcast_in_dim.24), channel_id=1, replica_groups=mesh['x'=4,'core'=2,'row'=8,'col'=4] {'x','col'}, dimensions={0} | all-to-all | bytes 65536 | tf_op jit(solution)/shard_map/all_to_all | solution.py:99
  136.3 9.2 %all_to_all.60 = f32[8,1,896]{2,1,0:T(1,128)S(1)} all-to-all(f32[8,1,896]{2,1,0:T(1,128)S(1)} %broadcast_in_dim.25), channel_id=1, replica_groups=mesh['x'=4,'core'=2,'row'=8,'col'=4] {'row'}, dimensions={0} | all-to-all | bytes 57344 | tf_op jit(solution)/shard_map/all_to_all | solution.py:99
  146.1 9.3 %all_to_all.61 = f32[16,1,512]{2,1,0:T(1,128)S(1)} all-to-all(f32[16,1,512]{2,1,0:T(1,128)S(1)} %broadcast_in_dim.26), channel_id=1, replica_groups=mesh['x'=4,'core'=2,'row'=8,'col'=4] {'x','col'}, dimensions={0} | all-to-all | bytes 65536 | tf_op jit(solution)/shard_map/all_to_all | solution.py:99
  156.0 9.5 %all_to_all.62 = f32[8,1,896]{2,1,0:T(1,128)S(1)} all-to-all(f32[8,1,896]{2,1,0:T(1,128)S(1)} %broadcast_in_dim.27), channel_id=1, replica_groups=mesh['x'=4,'core'=2,'row'=8,'col'=4] {'row'}, dimensions={0} | all-to-all | bytes 57344 | tf_op jit(solution)/shard_map/all_to_all | solution.py:99
  166.1 9.1 %all_to_all.63 = f32[16,1,512]{2,1,0:T(1,128)S(1)} all-to-all(f32[16,1,512]{2,1,0:T(1,128)S(1)} %broadcast_in_dim.28), channel_id=1, replica_groups=mesh['x'=4,'core'=2,'row'=8,'col'=4] {'x','col'}, dimensions={0} | all-to-all | bytes 65536 | tf_op jit(solution)/shard_map/all_to_all | solution.py:99
  175.9 9.2 %all_to_all.64 = f32[8,1,896]{2,1,0:T(1,128)S(1)} all-to-all(f32[8,1,896]{2,1,0:T(1,128)S(1)} %broadcast_in_dim.29), channel_id=1, replica_groups=mesh['x'=4,'core'=2,'row'=8,'col'=4] {'row'}, dimensions={0} | all-to-all | bytes 57344 | tf_op jit(solution)/shard_map/all_to_all | solution.py:99
  185.6 40.8 %all_to_all.65.pieces = f32[8,64,896]{2,1,0:T(8,128)S(1)} all-to-all(f32[8,64,896]{2,1,0:T(8,128)S(1)} %bitcast.16), channel_id=1, replica_groups=mesh['x'=4,'core'=2,'row'=8,'col'=4] {'x','core'}, dimensions={0} | all-to-all | bytes 3670016 | tf_op jit(solution)/shard_map/all_to_all | solution.py:150
  226.4 2.4 %shard_map.45 = (f32[2,64,3584]{2,1,0:T(8,128)}, f32[2,64,3584]{2,1,0:T(8,128)}) custom-call(f32[8,64,896]{2,1,0:T(8,128)S(1)} %all_to_all.65.pieces, f32[2,64,3584]{2,1,0:T(8,128)S(1)} %copy-done.1), custom_call_target="tpu_custom_call" | custom-call | tf_op jit(solution)/shard_map/pallas_call | solution.py:111
  (86 shorter events, 5.9 us)
Async XLA Ops:
  0.7 3.1 %copy-start = (bf16[1,2,8,64,3584]{4,3,2,1,0:T(8,128)(2,1)S(1)}, bf16[1,2,8,64,3584]{4,3,2,1,0:T(8,128)(2,1)}, u32[]{:S(2)}) copy-start(bf16[1,2,8,64,3584]{4,3,2,1,0:T(8,128)(2,1)} %param.2) | copy-start | bytes 22020100
  4.7 6.7 %collective-permute-start = (f32[1,2,4,64,896]{4,3,2,1,0:T(8,128)S(1)}, f32[1,2,4,64,896]{4,3,2,1,0:T(8,128)S(1)}, u32[]{:S(2)}, u32[]{:S(2)}) collective-permute-start(f32[1,2,4,64,896]{4,3,2,1,0:T(8,128)S(1)} %shard_map.41), channel_id=1, source_target_pairs={{0,32},{32,0},{1,33},{33,1},{2,34},{34,2},{3,35},{35,3},{4,36},{36... | collective-permute-start | bytes 5505032 | tf_op jit(solution)/shard_map/ppermute | solution.py:67
  14.1 9.1 %collective-permute-start.1 = (f32[3,2,4,64,896]{4,3,2,1,0:T(8,128)S(1)}, f32[3,2,4,64,896]{4,3,2,1,0:T(8,128)S(1)}, u32[]{:S(2)}, u32[]{:S(2)}) collective-permute-start(f32[3,2,4,64,896]{4,3,2,1,0:T(8,128)S(1)} %shard_map.43), channel_id=1, source_target_pairs={{0,32},{32,0},{1,33},{33,1},{2,34},{34,2},{3,35},{35,3},{4,36},{36... | collective-permute-start | bytes 16515080 | tf_op jit(solution)/shard_map/ppermute | solution.py:67
  14.6 23.0 %collective-permute-start.3 = (f32[4,64,896]{2,1,0:T(8,128)S(1)}, f32[4,64,896]{2,1,0:T(8,128)S(1)}, u32[]{:S(2)}, u32[]{:S(2)}) collective-permute-start(f32[4,64,896]{2,1,0:T(8,128)S(1)} %get-tuple-element.11), channel_id=1, source_target_pairs={{0,64},{64,128},{128,192},{192,0},{1,65},{65,129},{129,193},{193,1... | collective-permute-start | bytes 2752520 | tf_op jit(solution)/shard_map/ppermute | solution.py:71
  14.6 23.3 %collective-permute-start.6 = (f32[4,64,896]{2,1,0:T(8,128)S(1)}, f32[4,64,896]{2,1,0:T(8,128)S(1)}, u32[]{:S(2)}, u32[]{:S(2)}) collective-permute-start(f32[4,64,896]{2,1,0:T(8,128)S(1)} %get-tuple-element.19), channel_id=1, source_target_pairs={{0,192},{64,0},{128,64},{192,128},{1,193},{65,1},{129,65},{193,129... | collective-permute-start | bytes 2752520 | tf_op jit(solution)/shard_map/ppermute | solution.py:71
  25.8 30.4 %collective-permute-start.2 = (f32[4,64,896]{2,1,0:T(8,128)S(1)}, f32[4,64,896]{2,1,0:T(8,128)S(1)}, u32[]{:S(2)}, u32[]{:S(2)}) collective-permute-start(f32[4,64,896]{2,1,0:T(8,128)S(1)} %get-tuple-element.14), channel_id=1, source_target_pairs={{0,192},{64,0},{128,64},{192,128},{1,193},{65,1},{129,65},{193,129... | collective-permute-start | bytes 2752520 | tf_op jit(solution)/shard_map/ppermute | solution.py:71
  37.7 22.2 %collective-permute-start.4 = (f32[4,64,896]{2,1,0:T(8,128)S(1)}, f32[4,64,896]{2,1,0:T(8,128)S(1)}, u32[]{:S(2)}, u32[]{:S(2)}) collective-permute-start(f32[4,64,896]{2,1,0:T(8,128)S(1)} %add.147), channel_id=1, source_target_pairs={{0,64},{64,128},{128,192},{192,0},{1,65},{65,129},{129,193},{193,1... | collective-permute-start | bytes 2752520 | tf_op jit(solution)/shard_map/ppermute | solution.py:71
  37.8 41.9 %collective-permute-start.5 = (f32[4,64,896]{2,1,0:T(8,128)S(1)}, f32[4,64,896]{2,1,0:T(8,128)}, u32[]{:S(2)}, u32[]{:S(2)}) collective-permute-start(f32[4,64,896]{2,1,0:T(8,128)S(1)} %get-tuple-element.17), channel_id=1, source_target_pairs={{0,64},{64,128},{128,192},{192,0},{1,65},{65,129},{129,193},{193,1... | collective-permute-start | bytes 2752520 | tf_op jit(solution)/shard_map/ppermute | solution.py:71
  39.0 40.7 %collective-permute-start.7 = (f32[4,64,896]{2,1,0:T(8,128)}, f32[4,64,896]{2,1,0:T(8,128)}, u32[]{:S(2)}, u32[]{:S(2)}) collective-permute-start(f32[4,64,896]{2,1,0:T(8,128)} %add.150), channel_id=1, source_target_pairs={{0,192},{64,0},{128,64},{192,128},{1,193},{65,1},{129,65},{193,129... | collective-permute-start | bytes 2752520 | tf_op jit(solution)/shard_map/ppermute | solution.py:71
  185.6 40.8 %copy-start.1 = (f32[2,64,3584]{2,1,0:T(8,128)S(1)}, f32[2,64,3584]{2,1,0:T(8,128)}, u32[]{:S(2)}) copy-start(f32[2,64,3584]{2,1,0:T(8,128)} %weights.1) | copy-start | bytes 5505028

commit v4 on v3

--- a/solution.py
+++ b/solution.py
@@ -128,8 +128,9 @@
     halves = reduce_scatter(grads, place, size_x)
     width = columns // size_x
 
-    values = [h.reshape(size_x * rows, width) for h in halves]
-    row_factor = jnp.ones((CORES, size_x * rows), jnp.float32)
+    halves = lax.optimization_barrier(halves)
+    values = [jnp.concatenate(halves).reshape(blocks * rows, width)]
+    row_factor = jnp.ones((1, blocks * rows), jnp.float32)
     column_factor = jnp.ones((width,), jnp.float32)
 
     def scaled():
@@ -140,12 +141,12 @@
     for sweep in range(ITERS):
         part = jnp.concatenate([jnp.sum(v * v, axis=1) for v in scaled()])
         total = group_sum(part, ("x", "col"), size_x * size_col)
-        row_factor = row_factor * lax.rsqrt(total / FW + EPSILON).reshape(CORES, -1)
+        row_factor = row_factor * lax.rsqrt(total / FW + EPSILON).reshape(1, -1)
         part = sum(jnp.sum(v * v, axis=0) for v in scaled())
         total = group_sum(part, ("row",), size_row)
         column_factor = column_factor * lax.rsqrt(total / DW + EPSILON)
 
-    direction = jnp.stack([v.reshape(size_x, rows, width) for v in scaled()], axis=1)
+    direction = scaled()[0].reshape(CORES, size_x, rows, width).transpose(1, 0, 2, 3)
     direction = direction.reshape(blocks, rows, width)
     direction = lax.all_to_all(direction, ("x", "core"), 0, 0, tiled=True)
     return update(direction, weights)

time: 229 us -> 228 us (level)
  blocking collectives: 139 us -> 130 us
  waiting for transfers between devices: 58.1 us -> 65.7 us
  starting transfers between devices: 10.1 us -> 13.5 us
  other arithmetic: 7.21 us -> 4.47 us
    all_to_all x10 -> x9, blocking collectives: 98 us -> 88.9 us  [group_sum(): return jnp.sum(lax.all_to_all(spread, axes, 0, 0, tiled=True), axis=(0, 1))]
    all_to_all x0 -> x1, waiting for transfers between devices: none -> 6.66 us  [group_sum(): return jnp.sum(lax.all_to_all(spread, axes, 0, 0, tiled=True), axis=(0, 1))]
    all_to_all x0 -> x1, starting transfers between devices: none -> 3.34 us  [group_sum(): return jnp.sum(lax.all_to_all(spread, axes, 0, 0, tiled=True), axis=(0, 1))]
  transfers between devices with their start and end apart: 8 -> 9, of which waited for: 6 -> 7; matrix products, arithmetic and copies ran while one was open for 1% -> 0% of each run, Pallas kernels for 1% -> 1%
where the time goes in v4:
time: 228 us
  blocking collectives  130 us (57%)
  waiting for transfers between devices  65.7 us (29%)
  starting transfers between devices  13.5 us (6%)
  Pallas kernels  8.55 us (4%)
  local copies, waits for them, and re-layouts  4.87 us (2%)
  other arithmetic  4.47 us (2%)
    all_to_all x9, blocking collectives, group_sum(): return jnp.sum(lax.all_to_all(spread, axes, 0, 0, tiled=True), axis=(0, 1))  88.9 us
    ppermute x6, waiting for transfers between devices, move(): lax.ppermute(values, 'x', [(i, (i + step) % size) for i in range(size)])  49.6 us
    all_to_all x1, blocking collectives, per_device(): direction = lax.all_to_all(direction, ('x', 'core'), 0, 0, tiled=True)  40.7 us
    ppermute x2, waiting for transfers between devices, swap(): return lax.ppermute(values, 'core', [(0, 1), (1, 0)])  9.39 us
    all_to_all x1, waiting for transfers between devices, group_sum(): return jnp.sum(lax.all_to_all(spread, axes, 0, 0, tiled=True), axis=(0, 1))  6.66 us
    ppermute x6, starting transfers between devices, move(): lax.ppermute(values, 'x', [(i, (i + step) % size) for i in range(size)])  6.39 us
    pallas_call x4, Pallas kernels, widen(): pl.pallas_call(functools.partial(widen_kernel, count, own), grid_spec=plt...  6.16 us
  transfers between devices with their start and end apart: 9, of which 7 were waited for; matrix products, arithmetic and copies ran while one was open for 0% of the time, Pallas kernels for 1%

profile of v4, /device:TPU:1, one launch (start us, length us, event | category | flops | bytes accessed | tf_op | source)
XLA Modules:
  0.0 227.7 jit_solution(12543366507778822731)
XLA Ops:
  0.7 3.1 %copy-done = bf16[1,2,8,64,3584]{4,3,2,1,0:T(8,128)(2,1)S(1)} copy-done((bf16[1,2,8,64,3584]{4,3,2,1,0:T(8,128)(2,1)S(1)}, bf16[1,2,8,64,3584]{4,3,2,1,0:T(8,128)(2,1)}, u32[]{:S(2)}) %copy-start) | copy-done | bytes 7340056
  3.8 0.9 shard_map.41
  4.7 3.3 %collective-permute-start = (f32[1,2,4,64,896]{4,3,2,1,0:T(8,128)S(1)}, f32[1,2,4,64,896]{4,3,2,1,0:T(8,128)S(1)}, u32[]{:S(2)}, u32[]{:S(2)}) collective-permute-start(f32[1,2,4,64,896]{4,3,2,1,0:T(8,128)S(1)} %shard_map.41), channel_id=1, source_target_pairs={{0,32},{32,0},{1,33},{33,1},{2,34},{34,2},{3,35},{35,3},{4,36},{36... | collective-permute-start | bytes 5505032 | tf_op jit(solution)/shard_map/ppermute | solution.py:67
  8.1 3.4 %collective-permute-done.refs_1_ = f32[1,2,4,64,896]{4,3,2,1,0:T(8,128)S(1)} collective-permute-done((f32[1,2,4,64,896]{4,3,2,1,0:T(8,128)S(1)}, f32[1,2,4,64,896]{4,3,2,1,0:T(8,128)S(1)}, u32[]{:S(2)}, u32[]{:S(2)}) %collective-permute-start) | collective-permute-done | bytes 1835040 | tf_op jit(solution)/shard_map/ppermute | solution.py:67
  11.5 1.0 shard_map.42
  12.5 1.6 shard_map.43
  14.1 0.5 collective-permute-start.1
  14.6 2.7 %collective-permute-start.6 = (f32[4,64,896]{2,1,0:T(8,128)S(1)}, f32[4,64,896]{2,1,0:T(8,128)S(1)}, u32[]{:S(2)}, u32[]{:S(2)}) collective-permute-start(f32[4,64,896]{2,1,0:T(8,128)S(1)} %get-tuple-element.21), channel_id=1, source_target_pairs={{0,192},{64,0},{128,64},{192,128},{1,193},{65,1},{129,65},{193,129... | collective-permute-start | bytes 2752520 | tf_op jit(solution)/shard_map/ppermute | solution.py:71
  17.2 6.0 %collective-permute-done.1.refs_3_ = f32[3,2,4,64,896]{4,3,2,1,0:T(8,128)S(1)} collective-permute-done((f32[3,2,4,64,896]{4,3,2,1,0:T(8,128)S(1)}, f32[3,2,4,64,896]{4,3,2,1,0:T(8,128)S(1)}, u32[]{:S(2)}, u32[]{:S(2)}) %collective-permute-start.1) | collective-permute-done | bytes 5505056 | tf_op jit(solution)/shard_map/ppermute | solution.py:67
  23.2 2.6 %shard_map.44 = (f32[4,64,896]{2,1,0:T(8,128)S(1)}, f32[4,64,896]{2,1,0:T(8,128)S(1)}, f32[4,64,896]{2,1,0:T(8,128)S(1)}, f32[4,64,896]{2,1,0:T(8,128)S(1)}, f32...) custom-call(s32[2]{0:T(128)S(1)} %pad_add_fusion.place, bf16[2,4,2,64,3584]{4,3,2,1,0:T(8,128)(2,1)} %bitcast.7, ...), custom_call_target="tpu_custom_call" | custom-call | tf_op jit(solution)/shard_map/pallas_call | solution.py:53
  25.8 0.8 collective-permute-start.2
  26.7 10.9 %collective-permute-done.3 = f32[4,64,896]{2,1,0:T(8,128)S(1)} collective-permute-done((f32[4,64,896]{2,1,0:T(8,128)S(1)}, f32[4,64,896]{2,1,0:T(8,128)S(1)}, u32[]{:S(2)}, u32[]{:S(2)}) %collective-permute-start.3) | collective-permute-done | bytes 917536 | tf_op jit(solution)/shard_map/ppermute | solution.py:71
  38.0 2.7 %collective-permute-start.7 = (f32[4,64,896]{2,1,0:T(8,128)S(1)}, f32[4,64,896]{2,1,0:T(8,128)S(1)}, u32[]{:S(2)}, u32[]{:S(2)}) collective-permute-start(f32[4,64,896]{2,1,0:T(8,128)S(1)} %add.181), channel_id=1, source_target_pairs={{0,192},{64,0},{128,64},{192,128},{1,193},{65,1},{129,65},{193,129... | collective-permute-start | bytes 2752520 | tf_op jit(solution)/shard_map/ppermute | solution.py:71
  40.7 15.5 %collective-permute-done.2 = f32[4,64,896]{2,1,0:T(8,128)S(1)} collective-permute-done((f32[4,64,896]{2,1,0:T(8,128)S(1)}, f32[4,64,896]{2,1,0:T(8,128)S(1)}, u32[]{:S(2)}, u32[]{:S(2)}) %collective-permute-start.2) | collective-permute-done | bytes 917536 | tf_op jit(solution)/shard_map/ppermute | solution.py:71
  56.2 3.7 %collective-permute-done.4 = f32[4,64,896]{2,1,0:T(8,128)S(1)} collective-permute-done((f32[4,64,896]{2,1,0:T(8,128)S(1)}, f32[4,64,896]{2,1,0:T(8,128)S(1)}, u32[]{:S(2)}, u32[]{:S(2)}) %collective-permute-start.4) | collective-permute-done | bytes 917536 | tf_op jit(solution)/shard_map/ppermute | solution.py:71
  60.0 19.5 %collective-permute-done.5 = f32[4,64,896]{2,1,0:T(8,128)S(1)} collective-permute-done((f32[4,64,896]{2,1,0:T(8,128)S(1)}, f32[4,64,896]{2,1,0:T(8,128)S(1)}, u32[]{:S(2)}, u32[]{:S(2)}) %collective-permute-start.5) | collective-permute-done | bytes 917536 | tf_op jit(solution)/shard_map/ppermute | solution.py:71
  80.1 9.0 %all_to_all.55 = f32[16,1,512]{2,1,0:T(1,128)S(1)} all-to-all(f32[16,1,512]{2,1,0:T(1,128)S(1)} %broadcast_in_dim.31), channel_id=1, replica_groups=mesh['x'=4,'core'=2,'row'=8,'col'=4] {'x','col'}, dimensions={0} | all-to-all | bytes 65536 | tf_op jit(solution)/shard_map/all_to_all | solution.py:99
  89.6 14.7 %all_to_all.56 = f32[8,1,896]{2,1,0:T(1,128)S(1)} all-to-all(f32[8,1,896]{2,1,0:T(1,128)S(1)} %broadcast_in_dim.32), channel_id=1, replica_groups=mesh['x'=4,'core'=2,'row'=8,'col'=4] {'row'}, dimensions={0} | all-to-all | bytes 57344 | tf_op jit(solution)/shard_map/all_to_all | solution.py:99
  104.3 0.4 multiply_reduce_fusion.7
  104.8 9.6 %all_to_all.57 = f32[16,1,512]{2,1,0:T(1,128)S(1)} all-to-all(f32[16,1,512]{2,1,0:T(1,128)S(1)} %broadcast_in_dim.34), channel_id=1, replica_groups=mesh['x'=4,'core'=2,'row'=8,'col'=4] {'x','col'}, dimensions={0} | all-to-all | bytes 65536 | tf_op jit(solution)/shard_map/all_to_all | solution.py:99
  114.8 9.2 %all_to_all.58 = f32[8,1,896]{2,1,0:T(1,128)S(1)} all-to-all(f32[8,1,896]{2,1,0:T(1,128)S(1)} %broadcast_in_dim.35), channel_id=1, replica_groups=mesh['x'=4,'core'=2,'row'=8,'col'=4] {'row'}, dimensions={0} | all-to-all | bytes 57344 | tf_op jit(solution)/shard_map/all_to_all | solution.py:99
  124.6 9.3 %all_to_all.59 = f32[16,1,512]{2,1,0:T(1,128)S(1)} all-to-all(f32[16,1,512]{2,1,0:T(1,128)S(1)} %broadcast_in_dim.37), channel_id=1, replica_groups=mesh['x'=4,'core'=2,'row'=8,'col'=4] {'x','col'}, dimensions={0} | all-to-all | bytes 65536 | tf_op jit(solution)/shard_map/all_to_all | solution.py:99
  134.3 9.2 %all_to_all.60 = f32[8,1,896]{2,1,0:T(1,128)S(1)} all-to-all(f32[8,1,896]{2,1,0:T(1,128)S(1)} %broadcast_in_dim.38), channel_id=1, replica_groups=mesh['x'=4,'core'=2,'row'=8,'col'=4] {'row'}, dimensions={0} | all-to-all | bytes 57344 | tf_op jit(solution)/shard_map/all_to_all | solution.py:99
  143.6 0.4 multiply_reduce_fusion.3
  144.1 9.3 %all_to_all.61 = f32[16,1,512]{2,1,0:T(1,128)S(1)} all-to-all(f32[16,1,512]{2,1,0:T(1,128)S(1)} %broadcast_in_dim.40), channel_id=1, replica_groups=mesh['x'=4,'core'=2,'row'=8,'col'=4] {'x','col'}, dimensions={0} | all-to-all | bytes 65536 | tf_op jit(solution)/shard_map/all_to_all | solution.py:99
  153.8 9.2 %all_to_all.62 = f32[8,1,896]{2,1,0:T(1,128)S(1)} all-to-all(f32[8,1,896]{2,1,0:T(1,128)S(1)} %broadcast_in_dim.41), channel_id=1, replica_groups=mesh['x'=4,'core'=2,'row'=8,'col'=4] {'row'}, dimensions={0} | all-to-all | bytes 57344 | tf_op jit(solution)/shard_map/all_to_all | solution.py:99
  163.6 9.5 %all_to_all.63 = f32[16,1,512]{2,1,0:T(1,128)S(1)} all-to-all(f32[16,1,512]{2,1,0:T(1,128)S(1)} %broadcast_in_dim.43), channel_id=1, replica_groups=mesh['x'=4,'core'=2,'row'=8,'col'=4] {'x','col'}, dimensions={0} | all-to-all | bytes 65536 | tf_op jit(solution)/shard_map/all_to_all | solution.py:99
  173.5 0.6 broadcast_in_dim.44
  174.1 3.3 %all-to-all-start.9 = ((f32[8,1,896]{2,1,0:T(1,128)}), f32[8,1,896]{2,1,0:T(1,128)S(1)}, u32[]{:S(2)}, u32[]{:S(2)}) async-start(f32[8,1,896]{2,1,0:T(1,128)} %broadcast_in_dim.44), calls=%async_computation.9 | async-start | bytes 57344 | tf_op jit(solution)/shard_map/all_to_all | solution.py:99
  177.6 6.7 %all-to-all-done.9 = f32[8,1,896]{2,1,0:T(1,128)S(1)} async-done(((f32[8,1,896]{2,1,0:T(1,128)}), f32[8,1,896]{2,1,0:T(1,128)S(1)}, u32[]{:S(2)}, u32[]{:S(2)}) %all-to-all-start.9) | async-done | bytes 28704 | tf_op jit(solution)/shard_map/all_to_all | solution.py:99
  184.5 40.7 %all_to_all.64.pieces = f32[8,64,896]{2,1,0:T(8,128)S(1)} all-to-all(f32[8,64,896]{2,1,0:T(8,128)S(1)} %bitcast.16), channel_id=1, replica_groups=mesh['x'=4,'core'=2,'row'=8,'col'=4] {'x','core'}, dimensions={0} | all-to-all | bytes 3670016 | tf_op jit(solution)/shard_map/all_to_all | solution.py:151
  225.3 2.4 %shard_map.45 = (f32[2,64,3584]{2,1,0:T(8,128)}, f32[2,64,3584]{2,1,0:T(8,128)}) custom-call(f32[8,64,896]{2,1,0:T(8,128)S(1)} %all_to_all.64.pieces, f32[2,64,3584]{2,1,0:T(8,128)S(1)} %copy-done.1), custom_call_target="tpu_custom_call" | custom-call | tf_op jit(solution)/shard_map/pallas_call | solution.py:111
  (69 shorter events, 5.0 us)
Async XLA Ops:
  0.7 3.1 %copy-start = (bf16[1,2,8,64,3584]{4,3,2,1,0:T(8,128)(2,1)S(1)}, bf16[1,2,8,64,3584]{4,3,2,1,0:T(8,128)(2,1)}, u32[]{:S(2)}) copy-start(bf16[1,2,8,64,3584]{4,3,2,1,0:T(8,128)(2,1)} %param.2) | copy-start | bytes 22020100
  4.7 6.7 %collective-permute-start = (f32[1,2,4,64,896]{4,3,2,1,0:T(8,128)S(1)}, f32[1,2,4,64,896]{4,3,2,1,0:T(8,128)S(1)}, u32[]{:S(2)}, u32[]{:S(2)}) collective-permute-start(f32[1,2,4,64,896]{4,3,2,1,0:T(8,128)S(1)} %shard_map.41), channel_id=1, source_target_pairs={{0,32},{32,0},{1,33},{33,1},{2,34},{34,2},{3,35},{35,3},{4,36},{36... | collective-permute-start | bytes 5505032 | tf_op jit(solution)/shard_map/ppermute | solution.py:67
  14.1 9.1 %collective-permute-start.1 = (f32[3,2,4,64,896]{4,3,2,1,0:T(8,128)S(1)}, f32[3,2,4,64,896]{4,3,2,1,0:T(8,128)S(1)}, u32[]{:S(2)}, u32[]{:S(2)}) collective-permute-start(f32[3,2,4,64,896]{4,3,2,1,0:T(8,128)S(1)} %shard_map.43), channel_id=1, source_target_pairs={{0,32},{32,0},{1,33},{33,1},{2,34},{34,2},{3,35},{35,3},{4,36},{36... | collective-permute-start | bytes 16515080 | tf_op jit(solution)/shard_map/ppermute | solution.py:67
  14.6 23.0 %collective-permute-start.3 = (f32[4,64,896]{2,1,0:T(8,128)S(1)}, f32[4,64,896]{2,1,0:T(8,128)S(1)}, u32[]{:S(2)}, u32[]{:S(2)}) collective-permute-start(f32[4,64,896]{2,1,0:T(8,128)S(1)} %get-tuple-element.13), channel_id=1, source_target_pairs={{0,64},{64,128},{128,192},{192,0},{1,65},{65,129},{129,193},{193,1... | collective-permute-start | bytes 2752520 | tf_op jit(solution)/shard_map/ppermute | solution.py:71
  14.6 23.3 %collective-permute-start.6 = (f32[4,64,896]{2,1,0:T(8,128)S(1)}, f32[4,64,896]{2,1,0:T(8,128)S(1)}, u32[]{:S(2)}, u32[]{:S(2)}) collective-permute-start(f32[4,64,896]{2,1,0:T(8,128)S(1)} %get-tuple-element.21), channel_id=1, source_target_pairs={{0,192},{64,0},{128,64},{192,128},{1,193},{65,1},{129,65},{193,129... | collective-permute-start | bytes 2752520 | tf_op jit(solution)/shard_map/ppermute | solution.py:71
  25.8 30.4 %collective-permute-start.2 = (f32[4,64,896]{2,1,0:T(8,128)S(1)}, f32[4,64,896]{2,1,0:T(8,128)S(1)}, u32[]{:S(2)}, u32[]{:S(2)}) collective-permute-start(f32[4,64,896]{2,1,0:T(8,128)S(1)} %get-tuple-element.16), channel_id=1, source_target_pairs={{0,192},{64,0},{128,64},{192,128},{1,193},{65,1},{129,65},{193,129... | collective-permute-start | bytes 2752520 | tf_op jit(solution)/shard_map/ppermute | solution.py:71
  37.7 22.2 %collective-permute-start.4 = (f32[4,64,896]{2,1,0:T(8,128)S(1)}, f32[4,64,896]{2,1,0:T(8,128)S(1)}, u32[]{:S(2)}, u32[]{:S(2)}) collective-permute-start(f32[4,64,896]{2,1,0:T(8,128)S(1)} %add.178), channel_id=1, source_target_pairs={{0,64},{64,128},{128,192},{192,0},{1,65},{65,129},{129,193},{193,1... | collective-permute-start | bytes 2752520 | tf_op jit(solution)/shard_map/ppermute | solution.py:71
  37.8 41.8 %collective-permute-start.5 = (f32[4,64,896]{2,1,0:T(8,128)S(1)}, f32[4,64,896]{2,1,0:T(8,128)S(1)}, u32[]{:S(2)}, u32[]{:S(2)}) collective-permute-start(f32[4,64,896]{2,1,0:T(8,128)S(1)} %get-tuple-element.19), channel_id=1, source_target_pairs={{0,64},{64,128},{128,192},{192,0},{1,65},{65,129},{129,193},{193,1... | collective-permute-start | bytes 2752520 | tf_op jit(solution)/shard_map/ppermute | solution.py:71
  38.0 41.6 %collective-permute-start.7 = (f32[4,64,896]{2,1,0:T(8,128)S(1)}, f32[4,64,896]{2,1,0:T(8,128)S(1)}, u32[]{:S(2)}, u32[]{:S(2)}) collective-permute-start(f32[4,64,896]{2,1,0:T(8,128)S(1)} %add.181), channel_id=1, source_target_pairs={{0,192},{64,0},{128,64},{192,128},{1,193},{65,1},{129,65},{193,129... | collective-permute-start | bytes 2752520 | tf_op jit(solution)/shard_map/ppermute | solution.py:71
  174.1 10.1 %all-to-all-start.9 = ((f32[8,1,896]{2,1,0:T(1,128)}), f32[8,1,896]{2,1,0:T(1,128)S(1)}, u32[]{:S(2)}, u32[]{:S(2)}) async-start(f32[8,1,896]{2,1,0:T(1,128)} %broadcast_in_dim.44), calls=%async_computation.9 | async-start | bytes 57344 | tf_op jit(solution)/shard_map/all_to_all | solution.py:99
  184.5 40.7 %copy-start.1 = (f32[2,64,3584]{2,1,0:T(8,128)S(1)}, f32[2,64,3584]{2,1,0:T(8,128)}, u32[]{:S(2)}) copy-start(f32[2,64,3584]{2,1,0:T(8,128)} %weights.1) | copy-start | bytes 5505028

commit v5 on v4

--- a/solution.py
+++ b/solution.py
@@ -76,14 +76,15 @@
 
 
 def reduce_scatter(grads, place, size):
-    def total(steps, place):
-        other = swap(widen(grads, place, size, steps)[0])
-        return widen(grads, place, size, steps, other)
+    def total(steps, sent):
+        return widen(grads, place, size, steps, swap(sent))
 
-    far_first, far_second = total((2,), place)
+    (sent,) = widen(grads, place, size, (2,))
+    (sent_later,) = widen(grads, after(place, sent), size, (1, 3, 0))
+    far_first, far_second = total((2,), sent)
     right = move(far_first, size, 1)
     left = move(far_second, size, -1)
-    parts = total((1, 3, 0), after(place, far_first))
+    parts = total((1, 3, 0), after(sent_later, far_first))
     next_first, next_second, last_first, last_second, first, second = parts
     right_plain = move(next_second, size, 1)
     left_plain = move(last_first, size, -1)

time: 228 us -> 227 us (level)
  transfers between devices with their start and end apart: 9 -> 9, of which waited for: 7 -> 7; matrix products, arithmetic and copies ran while one was open for 0% -> 0% of each run, Pallas kernels for 1% -> 2%
where the time goes in v5:
time: 227 us; the launch traced here: 226 us
  blocking collectives  130 us (57%)
  waiting for transfers between devices  64 us (28%)
  starting transfers between devices  13.5 us (6%)
  Pallas kernels  8.55 us (4%)
  local copies, waits for them, and re-layouts  4.87 us (2%)
  other arithmetic  4.53 us (2%)
    all_to_all x9, blocking collectives, group_sum(): return jnp.sum(lax.all_to_all(spread, axes, 0, 0, tiled=True), axis=(0, 1))  88.9 us
    ppermute x6, waiting for transfers between devices, move(): lax.ppermute(values, 'x', [(i, (i + step) % size) for i in range(size)])  49.6 us
    all_to_all x1, blocking collectives, per_device(): direction = lax.all_to_all(direction, ('x', 'core'), 0, 0, tiled=True)  40.7 us
    ppermute x2, waiting for transfers between devices, swap(): return lax.ppermute(values, 'core', [(0, 1), (1, 0)])  7.76 us
    all_to_all x1, waiting for transfers between devices, group_sum(): return jnp.sum(lax.all_to_all(spread, axes, 0, 0, tiled=True), axis=(0, 1))  6.66 us
    ppermute x6, starting transfers between devices, move(): lax.ppermute(values, 'x', [(i, (i + step) % size) for i in range(size)])  6.39 us
    pallas_call x4, Pallas kernels, widen(): pl.pallas_call(functools.partial(widen_kernel, count, own), grid_spec=plt...  6.15 us
  transfers between devices with their start and end apart: 9, of which 7 were waited for; matrix products, arithmetic and copies ran while one was open for 0% of the time, Pallas kernels for 2%

profile of v5, /device:TPU:1, one launch (start us, length us, event | category | flops | bytes accessed | tf_op | source)
XLA Modules:
  0.0 226.1 jit_solution(2286320040322159358)
XLA Ops:
  0.7 3.1 %copy-done = bf16[1,2,8,64,3584]{4,3,2,1,0:T(8,128)(2,1)S(1)} copy-done((bf16[1,2,8,64,3584]{4,3,2,1,0:T(8,128)(2,1)S(1)}, bf16[1,2,8,64,3584]{4,3,2,1,0:T(8,128)(2,1)}, u32[]{:S(2)}) %copy-start) | copy-done | bytes 7340056
  3.8 0.9 shard_map.41
  4.7 3.3 %collective-permute-start = (f32[1,2,4,64,896]{4,3,2,1,0:T(8,128)S(1)}, f32[1,2,4,64,896]{4,3,2,1,0:T(8,128)S(1)}, u32[]{:S(2)}, u32[]{:S(2)}) collective-permute-start(f32[1,2,4,64,896]{4,3,2,1,0:T(8,128)S(1)} %shard_map.41), channel_id=1, source_target_pairs={{0,32},{32,0},{1,33},{33,1},{2,34},{34,2},{3,35},{35,3},{4,36},{36... | collective-permute-start | bytes 5505032 | tf_op jit(solution)/shard_map/ppermute | solution.py:67
  8.1 1.6 shard_map.42
  9.7 1.8 collective-permute-done.refs_1_
  11.5 1.0 shard_map.43
  12.5 0.5 collective-permute-start.1
  12.9 2.7 %collective-permute-start.6 = (f32[4,64,896]{2,1,0:T(8,128)S(1)}, f32[4,64,896]{2,1,0:T(8,128)S(1)}, u32[]{:S(2)}, u32[]{:S(2)}) collective-permute-start(f32[4,64,896]{2,1,0:T(8,128)S(1)} %get-tuple-element.23), channel_id=1, source_target_pairs={{0,192},{64,0},{128,64},{192,128},{1,193},{65,1},{129,65},{193,129... | collective-permute-start | bytes 2752520 | tf_op jit(solution)/shard_map/ppermute | solution.py:71
  15.6 6.0 %collective-permute-done.1.refs_3_ = f32[3,2,4,64,896]{4,3,2,1,0:T(8,128)S(1)} collective-permute-done((f32[3,2,4,64,896]{4,3,2,1,0:T(8,128)S(1)}, f32[3,2,4,64,896]{4,3,2,1,0:T(8,128)S(1)}, u32[]{:S(2)}, u32[]{:S(2)}) %collective-permute-start.1) | collective-permute-done | bytes 5505056 | tf_op jit(solution)/shard_map/ppermute | solution.py:67
  21.6 2.6 %shard_map.44 = (f32[4,64,896]{2,1,0:T(8,128)S(1)}, f32[4,64,896]{2,1,0:T(8,128)S(1)}, f32[4,64,896]{2,1,0:T(8,128)S(1)}, f32[4,64,896]{2,1,0:T(8,128)S(1)}, f32...) custom-call(s32[2]{0:T(128)S(1)} %pad_add_fusion.place, bf16[2,4,2,64,3584]{4,3,2,1,0:T(8,128)(2,1)} %bitcast.7, ...), custom_call_target="tpu_custom_call" | custom-call | tf_op jit(solution)/shard_map/pallas_call | solution.py:53
  24.2 0.8 collective-permute-start.2
  25.0 10.9 %collective-permute-done.3 = f32[4,64,896]{2,1,0:T(8,128)S(1)} collective-permute-done((f32[4,64,896]{2,1,0:T(8,128)S(1)}, f32[4,64,896]{2,1,0:T(8,128)S(1)}, u32[]{:S(2)}, u32[]{:S(2)}) %collective-permute-start.3) | collective-permute-done | bytes 917536 | tf_op jit(solution)/shard_map/ppermute | solution.py:71
  36.3 2.7 %collective-permute-start.7 = (f32[4,64,896]{2,1,0:T(8,128)S(1)}, f32[4,64,896]{2,1,0:T(8,128)S(1)}, u32[]{:S(2)}, u32[]{:S(2)}) collective-permute-start(f32[4,64,896]{2,1,0:T(8,128)S(1)} %add.181), channel_id=1, source_target_pairs={{0,192},{64,0},{128,64},{192,128},{1,193},{65,1},{129,65},{193,129... | collective-permute-start | bytes 2752520 | tf_op jit(solution)/shard_map/ppermute | solution.py:71
  39.1 15.5 %collective-permute-done.2 = f32[4,64,896]{2,1,0:T(8,128)S(1)} collective-permute-done((f32[4,64,896]{2,1,0:T(8,128)S(1)}, f32[4,64,896]{2,1,0:T(8,128)S(1)}, u32[]{:S(2)}, u32[]{:S(2)}) %collective-permute-start.2) | collective-permute-done | bytes 917536 | tf_op jit(solution)/shard_map/ppermute | solution.py:71
  54.6 3.7 %collective-permute-done.4 = f32[4,64,896]{2,1,0:T(8,128)S(1)} collective-permute-done((f32[4,64,896]{2,1,0:T(8,128)S(1)}, f32[4,64,896]{2,1,0:T(8,128)S(1)}, u32[]{:S(2)}, u32[]{:S(2)}) %collective-permute-start.4) | collective-permute-done | bytes 917536 | tf_op jit(solution)/shard_map/ppermute | solution.py:71
  58.4 19.5 %collective-permute-done.5 = f32[4,64,896]{2,1,0:T(8,128)S(1)} collective-permute-done((f32[4,64,896]{2,1,0:T(8,128)S(1)}, f32[4,64,896]{2,1,0:T(8,128)S(1)}, u32[]{:S(2)}, u32[]{:S(2)}) %collective-permute-start.5) | collective-permute-done | bytes 917536 | tf_op jit(solution)/shard_map/ppermute | solution.py:71
  78.5 9.0 %all_to_all.55 = f32[16,1,512]{2,1,0:T(1,128)S(1)} all-to-all(f32[16,1,512]{2,1,0:T(1,128)S(1)} %broadcast_in_dim.31), channel_id=1, replica_groups=mesh['x'=4,'core'=2,'row'=8,'col'=4] {'x','col'}, dimensions={0} | all-to-all | bytes 65536 | tf_op jit(solution)/shard_map/all_to_all | solution.py:100
  88.0 14.7 %all_to_all.56 = f32[8,1,896]{2,1,0:T(1,128)S(1)} all-to-all(f32[8,1,896]{2,1,0:T(1,128)S(1)} %broadcast_in_dim.32), channel_id=1, replica_groups=mesh['x'=4,'core'=2,'row'=8,'col'=4] {'row'}, dimensions={0} | all-to-all | bytes 57344 | tf_op jit(solution)/shard_map/all_to_all | solution.py:100
  102.7 0.4 multiply_reduce_fusion.7
  103.2 9.6 %all_to_all.57 = f32[16,1,512]{2,1,0:T(1,128)S(1)} all-to-all(f32[16,1,512]{2,1,0:T(1,128)S(1)} %broadcast_in_dim.34), channel_id=1, replica_groups=mesh['x'=4,'core'=2,'row'=8,'col'=4] {'x','col'}, dimensions={0} | all-to-all | bytes 65536 | tf_op jit(solution)/shard_map/all_to_all | solution.py:100
  113.2 9.2 %all_to_all.58 = f32[8,1,896]{2,1,0:T(1,128)S(1)} all-to-all(f32[8,1,896]{2,1,0:T(1,128)S(1)} %broadcast_in_dim.35), channel_id=1, replica_groups=mesh['x'=4,'core'=2,'row'=8,'col'=4] {'row'}, dimensions={0} | all-to-all | bytes 57344 | tf_op jit(solution)/shard_map/all_to_all | solution.py:100
  123.0 9.3 %all_to_all.59 = f32[16,1,512]{2,1,0:T(1,128)S(1)} all-to-all(f32[16,1,512]{2,1,0:T(1,128)S(1)} %broadcast_in_dim.37), channel_id=1, replica_groups=mesh['x'=4,'core'=2,'row'=8,'col'=4] {'x','col'}, dimensions={0} | all-to-all | bytes 65536 | tf_op jit(solution)/shard_map/all_to_all | solution.py:100
  132.8 9.2 %all_to_all.60 = f32[8,1,896]{2,1,0:T(1,128)S(1)} all-to-all(f32[8,1,896]{2,1,0:T(1,128)S(1)} %broadcast_in_dim.38), channel_id=1, replica_groups=mesh['x'=4,'core'=2,'row'=8,'col'=4] {'row'}, dimensions={0} | all-to-all | bytes 57344 | tf_op jit(solution)/shard_map/all_to_all | solution.py:100
  142.0 0.4 multiply_reduce_fusion.3
  142.5 9.3 %all_to_all.61 = f32[16,1,512]{2,1,0:T(1,128)S(1)} all-to-all(f32[16,1,512]{2,1,0:T(1,128)S(1)} %broadcast_in_dim.40), channel_id=1, replica_groups=mesh['x'=4,'core'=2,'row'=8,'col'=4] {'x','col'}, dimensions={0} | all-to-all | bytes 65536 | tf_op jit(solution)/shard_map/all_to_all | solution.py:100
  152.3 9.2 %all_to_all.62 = f32[8,1,896]{2,1,0:T(1,128)S(1)} all-to-all(f32[8,1,896]{2,1,0:T(1,128)S(1)} %broadcast_in_dim.41), channel_id=1, replica_groups=mesh['x'=4,'core'=2,'row'=8,'col'=4] {'row'}, dimensions={0} | all-to-all | bytes 57344 | tf_op jit(solution)/shard_map/all_to_all | solution.py:100
  162.0 9.5 %all_to_all.63 = f32[16,1,512]{2,1,0:T(1,128)S(1)} all-to-all(f32[16,1,512]{2,1,0:T(1,128)S(1)} %broadcast_in_dim.43), channel_id=1, replica_groups=mesh['x'=4,'core'=2,'row'=8,'col'=4] {'x','col'}, dimensions={0} | all-to-all | bytes 65536 | tf_op jit(solution)/shard_map/all_to_all | solution.py:100
  171.9 0.6 broadcast_in_dim.44
  172.6 3.3 %all-to-all-start.9 = ((f32[8,1,896]{2,1,0:T(1,128)}), f32[8,1,896]{2,1,0:T(1,128)S(1)}, u32[]{:S(2)}, u32[]{:S(2)}) async-start(f32[8,1,896]{2,1,0:T(1,128)} %broadcast_in_dim.44), calls=%async_computation.9 | async-start | bytes 57344 | tf_op jit(solution)/shard_map/all_to_all | solution.py:100
  176.0 6.7 %all-to-all-done.9 = f32[8,1,896]{2,1,0:T(1,128)S(1)} async-done(((f32[8,1,896]{2,1,0:T(1,128)}), f32[8,1,896]{2,1,0:T(1,128)S(1)}, u32[]{:S(2)}, u32[]{:S(2)}) %all-to-all-start.9) | async-done | bytes 28704 | tf_op jit(solution)/shard_map/all_to_all | solution.py:100
  182.9 40.7 %all_to_all.64.pieces = f32[8,64,896]{2,1,0:T(8,128)S(1)} all-to-all(f32[8,64,896]{2,1,0:T(8,128)S(1)} %bitcast.16), channel_id=1, replica_groups=mesh['x'=4,'core'=2,'row'=8,'col'=4] {'x','core'}, dimensions={0} | all-to-all | bytes 3670016 | tf_op jit(solution)/shard_map/all_to_all | solution.py:152
  223.7 2.4 %shard_map.45 = (f32[2,64,3584]{2,1,0:T(8,128)}, f32[2,64,3584]{2,1,0:T(8,128)}) custom-call(f32[8,64,896]{2,1,0:T(8,128)S(1)} %all_to_all.64.pieces, f32[2,64,3584]{2,1,0:T(8,128)S(1)} %copy-done.1), custom_call_target="tpu_custom_call" | custom-call | tf_op jit(solution)/shard_map/pallas_call | solution.py:112
  (69 shorter events, 5.1 us)
Async XLA Ops:
  0.7 3.1 %copy-start = (bf16[1,2,8,64,3584]{4,3,2,1,0:T(8,128)(2,1)S(1)}, bf16[1,2,8,64,3584]{4,3,2,1,0:T(8,128)(2,1)}, u32[]{:S(2)}) copy-start(bf16[1,2,8,64,3584]{4,3,2,1,0:T(8,128)(2,1)} %param.2) | copy-start | bytes 22020100
  4.7 6.7 %collective-permute-start = (f32[1,2,4,64,896]{4,3,2,1,0:T(8,128)S(1)}, f32[1,2,4,64,896]{4,3,2,1,0:T(8,128)S(1)}, u32[]{:S(2)}, u32[]{:S(2)}) collective-permute-start(f32[1,2,4,64,896]{4,3,2,1,0:T(8,128)S(1)} %shard_map.41), channel_id=1, source_target_pairs={{0,32},{32,0},{1,33},{33,1},{2,34},{34,2},{3,35},{35,3},{4,36},{36... | collective-permute-start | bytes 5505032 | tf_op jit(solution)/shard_map/ppermute | solution.py:67
  12.5 9.1 %collective-permute-start.1 = (f32[3,2,4,64,896]{4,3,2,1,0:T(8,128)S(1)}, f32[3,2,4,64,896]{4,3,2,1,0:T(8,128)S(1)}, u32[]{:S(2)}, u32[]{:S(2)}) collective-permute-start(f32[3,2,4,64,896]{4,3,2,1,0:T(8,128)S(1)} %shard_map.42), channel_id=1, source_target_pairs={{0,32},{32,0},{1,33},{33,1},{2,34},{34,2},{3,35},{35,3},{4,36},{36... | collective-permute-start | bytes 16515080 | tf_op jit(solution)/shard_map/ppermute | solution.py:67
  12.9 23.0 %collective-permute-start.3 = (f32[4,64,896]{2,1,0:T(8,128)S(1)}, f32[4,64,896]{2,1,0:T(8,128)S(1)}, u32[]{:S(2)}, u32[]{:S(2)}) collective-permute-start(f32[4,64,896]{2,1,0:T(8,128)S(1)} %get-tuple-element.15), channel_id=1, source_target_pairs={{0,64},{64,128},{128,192},{192,0},{1,65},{65,129},{129,193},{193,1... | collective-permute-start | bytes 2752520 | tf_op jit(solution)/shard_map/ppermute | solution.py:71
  12.9 23.3 %collective-permute-start.6 = (f32[4,64,896]{2,1,0:T(8,128)S(1)}, f32[4,64,896]{2,1,0:T(8,128)S(1)}, u32[]{:S(2)}, u32[]{:S(2)}) collective-permute-start(f32[4,64,896]{2,1,0:T(8,128)S(1)} %get-tuple-element.23), channel_id=1, source_target_pairs={{0,192},{64,0},{128,64},{192,128},{1,193},{65,1},{129,65},{193,129... | collective-permute-start | bytes 2752520 | tf_op jit(solution)/shard_map/ppermute | solution.py:71
  24.2 30.4 %collective-permute-start.2 = (f32[4,64,896]{2,1,0:T(8,128)S(1)}, f32[4,64,896]{2,1,0:T(8,128)S(1)}, u32[]{:S(2)}, u32[]{:S(2)}) collective-permute-start(f32[4,64,896]{2,1,0:T(8,128)S(1)} %get-tuple-element.18), channel_id=1, source_target_pairs={{0,192},{64,0},{128,64},{192,128},{1,193},{65,1},{129,65},{193,129... | collective-permute-start | bytes 2752520 | tf_op jit(solution)/shard_map/ppermute | solution.py:71
  36.1 22.2 %collective-permute-start.4 = (f32[4,64,896]{2,1,0:T(8,128)S(1)}, f32[4,64,896]{2,1,0:T(8,128)S(1)}, u32[]{:S(2)}, u32[]{:S(2)}) collective-permute-start(f32[4,64,896]{2,1,0:T(8,128)S(1)} %add.178), channel_id=1, source_target_pairs={{0,64},{64,128},{128,192},{192,0},{1,65},{65,129},{129,193},{193,1... | collective-permute-start | bytes 2752520 | tf_op jit(solution)/shard_map/ppermute | solution.py:71
  36.1 41.8 %collective-permute-start.5 = (f32[4,64,896]{2,1,0:T(8,128)S(1)}, f32[4,64,896]{2,1,0:T(8,128)S(1)}, u32[]{:S(2)}, u32[]{:S(2)}) collective-permute-start(f32[4,64,896]{2,1,0:T(8,128)S(1)} %get-tuple-element.21), channel_id=1, source_target_pairs={{0,64},{64,128},{128,192},{192,0},{1,65},{65,129},{129,193},{193,1... | collective-permute-start | bytes 2752520 | tf_op jit(solution)/shard_map/ppermute | solution.py:71
  36.3 41.6 %collective-permute-start.7 = (f32[4,64,896]{2,1,0:T(8,128)S(1)}, f32[4,64,896]{2,1,0:T(8,128)S(1)}, u32[]{:S(2)}, u32[]{:S(2)}) collective-permute-start(f32[4,64,896]{2,1,0:T(8,128)S(1)} %add.181), channel_id=1, source_target_pairs={{0,192},{64,0},{128,64},{192,128},{1,193},{65,1},{129,65},{193,129... | collective-permute-start | bytes 2752520 | tf_op jit(solution)/shard_map/ppermute | solution.py:71
  172.6 10.1 %all-to-all-start.9 = ((f32[8,1,896]{2,1,0:T(1,128)}), f32[8,1,896]{2,1,0:T(1,128)S(1)}, u32[]{:S(2)}, u32[]{:S(2)}) async-start(f32[8,1,896]{2,1,0:T(1,128)} %broadcast_in_dim.44), calls=%async_computation.9 | async-start | bytes 57344 | tf_op jit(solution)/shard_map/all_to_all | solution.py:100
  182.9 40.7 %copy-start.1 = (f32[2,64,3584]{2,1,0:T(8,128)S(1)}, f32[2,64,3584]{2,1,0:T(8,128)}, u32[]{:S(2)}) copy-start(f32[2,64,3584]{2,1,0:T(8,128)} %weights.1) | copy-start | bytes 5505028

commit v6 on v5

--- a/solution.py
+++ b/solution.py
@@ -101,18 +101,18 @@
 
 
 def update_kernel(pieces, weights, updated, direction):
-    values = pieces[...]
+    values = pieces[:, 0]
     direction[...] = values
     updated[...] = weights[...] * (1.0 - LEARNING_RATE * DECAY_RATE) - LEARNING_RATE * values
 
 
 def update(pieces, weights):
-    _, rows, width = pieces.shape
+    _, size, rows, width = pieces.shape
     side = pl.BlockSpec((CORES, rows, width), lambda i: (0, 0, i))
     return pl.pallas_call(
         update_kernel,
-        grid=(pieces.shape[0] // CORES,),
-        in_specs=[pl.BlockSpec((CORES, rows, width), lambda i: (i, 0, 0)), side],
+        grid=(size,),
+        in_specs=[pl.BlockSpec((CORES, 1, rows, width), lambda i: (0, i, 0, 0)), side],
         out_specs=[side, side],
         out_shape=[jax.ShapeDtypeStruct(weights.shape, jnp.float32)] * 2,
         compiler_params=pltpu.CompilerParams(vmem_limit_bytes=40 * 2**20),
@@ -147,9 +147,9 @@
         total = group_sum(part, ("row",), size_row)
         column_factor = column_factor * lax.rsqrt(total / DW + EPSILON)
 
-    direction = scaled()[0].reshape(CORES, size_x, rows, width).transpose(1, 0, 2, 3)
-    direction = direction.reshape(blocks, rows, width)
-    direction = lax.all_to_all(direction, ("x", "core"), 0, 0, tiled=True)
+    direction = scaled()[0].reshape(blocks, rows, width)
+    direction = lax.all_to_all(direction, ("core", "x"), 0, 0, tiled=True)
+    direction = direction.reshape(CORES, size_x, rows, width)
     return update(direction, weights)
 
 

time: 227 us -> 225 us (level)
  blocking collectives: 130 us -> 139 us
  waiting for transfers between devices: 64 us -> 57.4 us
  starting transfers between devices: 13.5 us -> 10.2 us
    all_to_all x9 -> x10, blocking collectives: 88.9 us -> 98.1 us  [group_sum(): return jnp.sum(lax.all_to_all(spread, axes, 0, 0, tiled=True), axis=(0, 1))]
    all_to_all x1 -> x0, waiting for transfers between devices: 6.66 us -> none  [group_sum(): return jnp.sum(lax.all_to_all(spread, axes, 0, 0, tiled=True), axis=(0, 1))]
    all_to_all x1 -> x0, starting transfers between devices: 3.34 us -> none  [group_sum(): return jnp.sum(lax.all_to_all(spread, axes, 0, 0, tiled=True), axis=(0, 1))]
  transfers between devices with their start and end apart: 9 -> 8, of which waited for: 7 -> 6; matrix products, arithmetic and copies ran while one was open for 0% -> 0% of each run, Pallas kernels for 2% -> 2%
where the time goes in v6:
time: 225 us
  blocking collectives  139 us (62%)
  waiting for transfers between devices  57.4 us (26%)
  starting transfers between devices  10.2 us (5%)
  Pallas kernels  8.72 us (4%)
  other arithmetic  4.52 us (2%)
  local copies, waits for them, and re-layouts  4.18 us (2%)
    all_to_all x10, blocking collectives, group_sum(): return jnp.sum(lax.all_to_all(spread, axes, 0, 0, tiled=True), axis=(0, 1))  98.1 us
    ppermute x6, waiting for transfers between devices, move(): lax.ppermute(values, 'x', [(i, (i + step) % size) for i in range(size)])  49.6 us
    all_to_all x1, blocking collectives, per_device(): direction = lax.all_to_all(direction, ('core', 'x'), 0, 0, tiled=True)  40.5 us
    ppermute x2, waiting for transfers between devices, swap(): return lax.ppermute(values, 'core', [(0, 1), (1, 0)])  7.76 us
    ppermute x6, starting transfers between devices, move(): lax.ppermute(values, 'x', [(i, (i + step) % size) for i in range(size)])  6.39 us
    pallas_call x4, Pallas kernels, widen(): pl.pallas_call(functools.partial(widen_kernel, count, own), grid_spec=plt...  6.15 us
  transfers between devices with their start and end apart: 8, of which 6 were waited for; matrix products, arithmetic and copies ran while one was open for 0% of the time, Pallas kernels for 2%

profile of v6, /device:TPU:1, one launch (start us, length us, event | category | flops | bytes accessed | tf_op | source)
XLA Modules:
  0.0 224.5 jit_solution(5023248617171306031)
XLA Ops:
  0.7 3.1 %copy-done = bf16[1,2,8,64,3584]{4,3,2,1,0:T(8,128)(2,1)S(1)} copy-done((bf16[1,2,8,64,3584]{4,3,2,1,0:T(8,128)(2,1)S(1)}, bf16[1,2,8,64,3584]{4,3,2,1,0:T(8,128)(2,1)}, u32[]{:S(2)}) %copy-start) | copy-done | bytes 7340056
  3.8 0.9 shard_map.41
  4.7 3.3 %collective-permute-start = (f32[1,2,4,64,896]{4,3,2,1,0:T(8,128)S(1)}, f32[1,2,4,64,896]{4,3,2,1,0:T(8,128)S(1)}, u32[]{:S(2)}, u32[]{:S(2)}) collective-permute-start(f32[1,2,4,64,896]{4,3,2,1,0:T(8,128)S(1)} %shard_map.41), channel_id=1, source_target_pairs={{0,32},{32,0},{1,33},{33,1},{2,34},{34,2},{3,35},{35,3},{4,36},{36... | collective-permute-start | bytes 5505032 | tf_op jit(solution)/shard_map/ppermute | solution.py:67
  8.1 1.6 shard_map.42
  9.7 1.8 collective-permute-done.refs_1_
  11.5 1.0 shard_map.43
  12.5 0.5 collective-permute-start.1
  12.9 2.7 %collective-permute-start.6 = (f32[4,64,896]{2,1,0:T(8,128)S(1)}, f32[4,64,896]{2,1,0:T(8,128)S(1)}, u32[]{:S(2)}, u32[]{:S(2)}) collective-permute-start(f32[4,64,896]{2,1,0:T(8,128)S(1)} %get-tuple-element.23), channel_id=1, source_target_pairs={{0,192},{64,0},{128,64},{192,128},{1,193},{65,1},{129,65},{193,129... | collective-permute-start | bytes 2752520 | tf_op jit(solution)/shard_map/ppermute | solution.py:71
  15.6 6.0 %collective-permute-done.1.refs_3_ = f32[3,2,4,64,896]{4,3,2,1,0:T(8,128)S(1)} collective-permute-done((f32[3,2,4,64,896]{4,3,2,1,0:T(8,128)S(1)}, f32[3,2,4,64,896]{4,3,2,1,0:T(8,128)S(1)}, u32[]{:S(2)}, u32[]{:S(2)}) %collective-permute-start.1) | collective-permute-done | bytes 5505056 | tf_op jit(solution)/shard_map/ppermute | solution.py:67
  21.6 2.6 %shard_map.44 = (f32[4,64,896]{2,1,0:T(8,128)S(1)}, f32[4,64,896]{2,1,0:T(8,128)S(1)}, f32[4,64,896]{2,1,0:T(8,128)S(1)}, f32[4,64,896]{2,1,0:T(8,128)S(1)}, f32...) custom-call(s32[2]{0:T(128)S(1)} %pad_add_fusion.place, bf16[2,4,2,64,3584]{4,3,2,1,0:T(8,128)(2,1)} %bitcast.4, ...), custom_call_target="tpu_custom_call" | custom-call | tf_op jit(solution)/shard_map/pallas_call | solution.py:53
  24.2 0.8 collective-permute-start.2
  25.0 10.9 %collective-permute-done.3 = f32[4,64,896]{2,1,0:T(8,128)S(1)} collective-permute-done((f32[4,64,896]{2,1,0:T(8,128)S(1)}, f32[4,64,896]{2,1,0:T(8,128)S(1)}, u32[]{:S(2)}, u32[]{:S(2)}) %collective-permute-start.3) | collective-permute-done | bytes 917536 | tf_op jit(solution)/shard_map/ppermute | solution.py:71
  36.3 2.7 %collective-permute-start.7 = (f32[4,64,896]{2,1,0:T(8,128)S(1)}, f32[4,64,896]{2,1,0:T(8,128)S(1)}, u32[]{:S(2)}, u32[]{:S(2)}) collective-permute-start(f32[4,64,896]{2,1,0:T(8,128)S(1)} %add.171), channel_id=1, source_target_pairs={{0,192},{64,0},{128,64},{192,128},{1,193},{65,1},{129,65},{193,129... | collective-permute-start | bytes 2752520 | tf_op jit(solution)/shard_map/ppermute | solution.py:71
  39.1 15.5 %collective-permute-done.2 = f32[4,64,896]{2,1,0:T(8,128)S(1)} collective-permute-done((f32[4,64,896]{2,1,0:T(8,128)S(1)}, f32[4,64,896]{2,1,0:T(8,128)S(1)}, u32[]{:S(2)}, u32[]{:S(2)}) %collective-permute-start.2) | collective-permute-done | bytes 917536 | tf_op jit(solution)/shard_map/ppermute | solution.py:71
  54.6 3.7 %collective-permute-done.4 = f32[4,64,896]{2,1,0:T(8,128)S(1)} collective-permute-done((f32[4,64,896]{2,1,0:T(8,128)S(1)}, f32[4,64,896]{2,1,0:T(8,128)S(1)}, u32[]{:S(2)}, u32[]{:S(2)}) %collective-permute-start.4) | collective-permute-done | bytes 917536 | tf_op jit(solution)/shard_map/ppermute | solution.py:71
  58.4 19.5 %collective-permute-done.5 = f32[4,64,896]{2,1,0:T(8,128)S(1)} collective-permute-done((f32[4,64,896]{2,1,0:T(8,128)S(1)}, f32[4,64,896]{2,1,0:T(8,128)S(1)}, u32[]{:S(2)}, u32[]{:S(2)}) %collective-permute-start.5) | collective-permute-done | bytes 917536 | tf_op jit(solution)/shard_map/ppermute | solution.py:71
  78.5 9.0 %all_to_all.55 = f32[16,1,512]{2,1,0:T(1,128)S(1)} all-to-all(f32[16,1,512]{2,1,0:T(1,128)S(1)} %broadcast_in_dim.31), channel_id=1, replica_groups=mesh['x'=4,'core'=2,'row'=8,'col'=4] {'x','col'}, dimensions={0} | all-to-all | bytes 65536 | tf_op jit(solution)/shard_map/all_to_all | solution.py:100
  88.0 14.7 %all_to_all.56 = f32[8,1,896]{2,1,0:T(1,128)S(1)} all-to-all(f32[8,1,896]{2,1,0:T(1,128)S(1)} %broadcast_in_dim.32), channel_id=1, replica_groups=mesh['x'=4,'core'=2,'row'=8,'col'=4] {'row'}, dimensions={0} | all-to-all | bytes 57344 | tf_op jit(solution)/shard_map/all_to_all | solution.py:100
  102.7 0.4 multiply_reduce_fusion.7
  103.2 9.6 %all_to_all.57 = f32[16,1,512]{2,1,0:T(1,128)S(1)} all-to-all(f32[16,1,512]{2,1,0:T(1,128)S(1)} %broadcast_in_dim.34), channel_id=1, replica_groups=mesh['x'=4,'core'=2,'row'=8,'col'=4] {'x','col'}, dimensions={0} | all-to-all | bytes 65536 | tf_op jit(solution)/shard_map/all_to_all | solution.py:100
  113.2 9.2 %all_to_all.58 = f32[8,1,896]{2,1,0:T(1,128)S(1)} all-to-all(f32[8,1,896]{2,1,0:T(1,128)S(1)} %broadcast_in_dim.35), channel_id=1, replica_groups=mesh['x'=4,'core'=2,'row'=8,'col'=4] {'row'}, dimensions={0} | all-to-all | bytes 57344 | tf_op jit(solution)/shard_map/all_to_all | solution.py:100
  122.5 0.4 multiply_reduce_fusion.5
  123.0 9.3 %all_to_all.59 = f32[16,1,512]{2,1,0:T(1,128)S(1)} all-to-all(f32[16,1,512]{2,1,0:T(1,128)S(1)} %broadcast_in_dim.37), channel_id=1, replica_groups=mesh['x'=4,'core'=2,'row'=8,'col'=4] {'x','col'}, dimensions={0} | all-to-all | bytes 65536 | tf_op jit(solution)/shard_map/all_to_all | solution.py:100
  132.8 9.2 %all_to_all.60 = f32[8,1,896]{2,1,0:T(1,128)S(1)} all-to-all(f32[8,1,896]{2,1,0:T(1,128)S(1)} %broadcast_in_dim.38), channel_id=1, replica_groups=mesh['x'=4,'core'=2,'row'=8,'col'=4] {'row'}, dimensions={0} | all-to-all | bytes 57344 | tf_op jit(solution)/shard_map/all_to_all | solution.py:100
  142.0 0.4 multiply_reduce_fusion.3
  142.5 9.3 %all_to_all.61 = f32[16,1,512]{2,1,0:T(1,128)S(1)} all-to-all(f32[16,1,512]{2,1,0:T(1,128)S(1)} %broadcast_in_dim.40), channel_id=1, replica_groups=mesh['x'=4,'core'=2,'row'=8,'col'=4] {'x','col'}, dimensions={0} | all-to-all | bytes 65536 | tf_op jit(solution)/shard_map/all_to_all | solution.py:100
  152.3 9.2 %all_to_all.62 = f32[8,1,896]{2,1,0:T(1,128)S(1)} all-to-all(f32[8,1,896]{2,1,0:T(1,128)S(1)} %broadcast_in_dim.41), channel_id=1, replica_groups=mesh['x'=4,'core'=2,'row'=8,'col'=4] {'row'}, dimensions={0} | all-to-all | bytes 57344 | tf_op jit(solution)/shard_map/all_to_all | solution.py:100
  161.5 0.4 multiply_reduce_fusion.1
  162.0 9.5 %all_to_all.63 = f32[16,1,512]{2,1,0:T(1,128)S(1)} all-to-all(f32[16,1,512]{2,1,0:T(1,128)S(1)} %broadcast_in_dim.43), channel_id=1, replica_groups=mesh['x'=4,'core'=2,'row'=8,'col'=4] {'x','col'}, dimensions={0} | all-to-all | bytes 65536 | tf_op jit(solution)/shard_map/all_to_all | solution.py:100
  172.0 9.2 %all_to_all.64 = f32[8,1,896]{2,1,0:T(1,128)S(1)} all-to-all(f32[8,1,896]{2,1,0:T(1,128)S(1)} %broadcast_in_dim.44), channel_id=1, replica_groups=mesh['x'=4,'core'=2,'row'=8,'col'=4] {'row'}, dimensions={0} | all-to-all | bytes 57344 | tf_op jit(solution)/shard_map/all_to_all | solution.py:100
  181.4 40.5 %all_to_all.65 = f32[8,64,896]{2,1,0:T(8,128)S(1)} all-to-all(f32[8,64,896]{2,1,0:T(8,128)S(1)} %multiply_multiply_fusion), channel_id=1, replica_groups=mesh['x'=4,'core'=2,'row'=8,'col'=4] {'core','x'}, dimensions={0} | all-to-all | bytes 3670016 | tf_op jit(solution)/shard_map/all_to_all | solution.py:151
  222.0 2.6 %shard_map.45 = (f32[2,64,3584]{2,1,0:T(8,128)}, f32[2,64,3584]{2,1,0:T(8,128)}) custom-call(f32[2,4,64,896]{3,2,1,0:T(8,128)S(1)} %bitcast.12, f32[2,64,3584]{2,1,0:T(8,128)S(1)} %copy-done.1), custom_call_target="tpu_custom_call" | custom-call | tf_op jit(solution)/shard_map/pallas_call | solution.py:112
  (66 shorter events, 4.3 us)
Async XLA Ops:
  0.7 3.1 %copy-start = (bf16[1,2,8,64,3584]{4,3,2,1,0:T(8,128)(2,1)S(1)}, bf16[1,2,8,64,3584]{4,3,2,1,0:T(8,128)(2,1)}, u32[]{:S(2)}) copy-start(bf16[1,2,8,64,3584]{4,3,2,1,0:T(8,128)(2,1)} %param.2) | copy-start | bytes 22020100
  4.7 6.7 %collective-permute-start = (f32[1,2,4,64,896]{4,3,2,1,0:T(8,128)S(1)}, f32[1,2,4,64,896]{4,3,2,1,0:T(8,128)S(1)}, u32[]{:S(2)}, u32[]{:S(2)}) collective-permute-start(f32[1,2,4,64,896]{4,3,2,1,0:T(8,128)S(1)} %shard_map.41), channel_id=1, source_target_pairs={{0,32},{32,0},{1,33},{33,1},{2,34},{34,2},{3,35},{35,3},{4,36},{36... | collective-permute-start | bytes 5505032 | tf_op jit(solution)/shard_map/ppermute | solution.py:67
  12.5 9.1 %collective-permute-start.1 = (f32[3,2,4,64,896]{4,3,2,1,0:T(8,128)S(1)}, f32[3,2,4,64,896]{4,3,2,1,0:T(8,128)S(1)}, u32[]{:S(2)}, u32[]{:S(2)}) collective-permute-start(f32[3,2,4,64,896]{4,3,2,1,0:T(8,128)S(1)} %shard_map.42), channel_id=1, source_target_pairs={{0,32},{32,0},{1,33},{33,1},{2,34},{34,2},{3,35},{35,3},{4,36},{36... | collective-permute-start | bytes 16515080 | tf_op jit(solution)/shard_map/ppermute | solution.py:67
  12.9 23.0 %collective-permute-start.3 = (f32[4,64,896]{2,1,0:T(8,128)S(1)}, f32[4,64,896]{2,1,0:T(8,128)S(1)}, u32[]{:S(2)}, u32[]{:S(2)}) collective-permute-start(f32[4,64,896]{2,1,0:T(8,128)S(1)} %get-tuple-element.15), channel_id=1, source_target_pairs={{0,64},{64,128},{128,192},{192,0},{1,65},{65,129},{129,193},{193,1... | collective-permute-start | bytes 2752520 | tf_op jit(solution)/shard_map/ppermute | solution.py:71
  12.9 23.3 %collective-permute-start.6 = (f32[4,64,896]{2,1,0:T(8,128)S(1)}, f32[4,64,896]{2,1,0:T(8,128)S(1)}, u32[]{:S(2)}, u32[]{:S(2)}) collective-permute-start(f32[4,64,896]{2,1,0:T(8,128)S(1)} %get-tuple-element.23), channel_id=1, source_target_pairs={{0,192},{64,0},{128,64},{192,128},{1,193},{65,1},{129,65},{193,129... | collective-permute-start | bytes 2752520 | tf_op jit(solution)/shard_map/ppermute | solution.py:71
  24.2 30.4 %collective-permute-start.2 = (f32[4,64,896]{2,1,0:T(8,128)S(1)}, f32[4,64,896]{2,1,0:T(8,128)S(1)}, u32[]{:S(2)}, u32[]{:S(2)}) collective-permute-start(f32[4,64,896]{2,1,0:T(8,128)S(1)} %get-tuple-element.18), channel_id=1, source_target_pairs={{0,192},{64,0},{128,64},{192,128},{1,193},{65,1},{129,65},{193,129... | collective-permute-start | bytes 2752520 | tf_op jit(solution)/shard_map/ppermute | solution.py:71
  36.1 22.2 %collective-permute-start.4 = (f32[4,64,896]{2,1,0:T(8,128)S(1)}, f32[4,64,896]{2,1,0:T(8,128)S(1)}, u32[]{:S(2)}, u32[]{:S(2)}) collective-permute-start(f32[4,64,896]{2,1,0:T(8,128)S(1)} %add.168), channel_id=1, source_target_pairs={{0,64},{64,128},{128,192},{192,0},{1,65},{65,129},{129,193},{193,1... | collective-permute-start | bytes 2752520 | tf_op jit(solution)/shard_map/ppermute | solution.py:71
  36.1 41.8 %collective-permute-start.5 = (f32[4,64,896]{2,1,0:T(8,128)S(1)}, f32[4,64,896]{2,1,0:T(8,128)S(1)}, u32[]{:S(2)}, u32[]{:S(2)}) collective-permute-start(f32[4,64,896]{2,1,0:T(8,128)S(1)} %get-tuple-element.21), channel_id=1, source_target_pairs={{0,64},{64,128},{128,192},{192,0},{1,65},{65,129},{129,193},{193,1... | collective-permute-start | bytes 2752520 | tf_op jit(solution)/shard_map/ppermute | solution.py:71
  36.3 41.6 %collective-permute-start.7 = (f32[4,64,896]{2,1,0:T(8,128)S(1)}, f32[4,64,896]{2,1,0:T(8,128)S(1)}, u32[]{:S(2)}, u32[]{:S(2)}) collective-permute-start(f32[4,64,896]{2,1,0:T(8,128)S(1)} %add.171), channel_id=1, source_target_pairs={{0,192},{64,0},{128,64},{192,128},{1,193},{65,1},{129,65},{193,129... | collective-permute-start | bytes 2752520 | tf_op jit(solution)/shard_map/ppermute | solution.py:71
  181.4 40.5 %copy-start.1 = (f32[2,64,3584]{2,1,0:T(8,128)S(1)}, f32[2,64,3584]{2,1,0:T(8,128)}, u32[]{:S(2)}) copy-start(f32[2,64,3584]{2,1,0:T(8,128)} %weights.1) | copy-start | bytes 5505028
